TPU v7x, 128 devices: a whole 4x4x4 slice. The times are simulated.
128 devices in a mesh: front: 4 (over z_hi, core), tile: 32 (over z_lo, y, x).
Axes of the slice: x: 4, y: 4, z: 4 (z_hi: 2, z_lo: 2; z = z_hi * 2 + z_lo), core: 2. Of those that a mesh axis runs over, the one named last changes fastest.
Arguments:
- fronts: float32 [4, 32, 2048, 1024], P('front', 'tile')
- parents: bfloat16 [4, 32, 2048, 1024], P('front', 'tile'), may hold values from -3 to 3
- parent_of: int32 [4], replicated, may hold values from 0 to 3
- block_map: int32 [4, 48], replicated, may hold values from 0 to 63, as said below
Outputs:
- factor: bfloat16 [4, 32, 2048, 256], P('front', 'tile')
- merged: float32 [4, 32, 2048, 1024], P('front', 'tile')
Inputs may be any that keep to these rules, and one draw needn't show every extreme that they name: block_map[g, a] % 8 == a % 8, and the 48 entries of one front are distinct.
All inputs are finite; a program needn't handle non-finite values.
Results may differ from a plain program's by a relative error of at most 0.0032.
Values may be sent and summed in bfloat16 or wider, within the bound.
No kernel may reach another device: no remote copies, remote signals or barrier semaphores. Data moves between devices by JAX's collectives and lax.ppermute only.
A program may use at most 192 MiB of HBM per device.

v0:
```python
import functools

import jax
import jax.numpy as jnp
from jax import lax
from jax.experimental import pallas as pl
from jax.experimental.pallas import tpu as pltpu
from jax.sharding import PartitionSpec as P

BLK = 128
F32 = jnp.float32
BF16 = jnp.bfloat16
NN = (((1,), (0,)), ((), ()))
NT = (((1,), (1,)), ((), ()))


def dot(a, b, dims):
    return lax.dot_general(a, b, dims, preferred_element_type=F32)


def split(x):
    hi = x.astype(BF16)
    return hi, (x - hi.astype(F32)).astype(BF16)


def dot3(a, b, dims):
    return dot(a[0], b[0], dims) + (dot(a[0], b[1], dims) + dot(a[1], b[0], dims))


def dotp(a, b, dims):
    return dot3(split(a), split(b), dims)


def lane_of(x, lane):
    return jnp.broadcast_to(x[:, lane : lane + 1], (8, BLK))


def factor_block(rows, out_ref, out_row, out_col, T):
    S = list(rows)
    lanes = lax.broadcasted_iota(jnp.int32, (8, BLK), 1)
    subs = lax.broadcasted_iota(jnp.int32, (8, BLK), 0)
    G = [(lanes == subs + 8 * v).astype(F32) for v in range(16)]
    for v0 in range(16):
        far = v0 + 3 + (v0 + 3) % 2
        far = far if far <= 12 else 16
        C = {v: [lane_of(S[v], 8 * v0 + j) for j in range(8)] for v in range(v0, far)}
        at = 80 * (v0 % 2)
        for n, x in enumerate([*C[v0], S[v0], G[v0]]):
            T[at + 8 * n : at + 8 * n + 8, :] = x

        def spread_row(n, i):
            return T[pl.ds(at + 8 * n + i, 8, stride=0), :]

        d = [[spread_row(j, i) if i >= j else None for j in range(8)] for i in range(8)]
        Rs = [spread_row(8, i) for i in range(8)]
        Rg = [spread_row(9, i) for i in range(8)]
        Cn = list(C[v0 + 1]) if v0 < 15 else None
        m = [[None] * 8 for _ in range(8)]
        Us, Ug = [None] * 8, [None] * 8
        wrows = None
        for j in range(8):
            rs = lax.rsqrt(d[j][j])
            p = rs * rs
            w = Rg[j] * rs
            wrows = w if j == 0 else jnp.where(subs == j, w, wrows)
            for i in range(j + 1, 8):
                m[i][j] = d[i][j] * p
            for i in range(j + 1, 8):
                for k in range(j + 1, i + 1):
                    d[i][k] = d[i][k] - m[i][j] * d[k][j]
            Us[j] = Rs[j] * p
            Ug[j] = Rg[j] * p
            if Cn is not None:
                S[v0 + 1] = S[v0 + 1] - Cn[j] * Us[j]
                G[v0 + 1] = G[v0 + 1] - Cn[j] * Ug[j]
            for i in range(j + 1, 8):
                Rs[i] = Rs[i] - m[i][j] * Rs[j]
                Rg[i] = Rg[i] - m[i][j] * Rg[j]
                if Cn is not None:
                    Cn[i] = Cn[i] - m[i][j] * Cn[j]
        out_ref[pl.ds(out_row + 8 * v0, 8), pl.ds(out_col, BLK)] = wrows
        if v0 < 14:
            for j in range(6, -1, -1):
                for i in range(j + 1, 8):
                    Us[j] = Us[j] - m[i][j] * Us[i]
                    Ug[j] = Ug[j] - m[i][j] * Ug[i]
            for v in range(v0 + 2, far):
                for j in range(8):
                    S[v] = S[v] - C[v][j] * Us[j]
                    G[v] = G[v] - C[v][j] * Ug[j]
            if far < 16:
                us, ug = Us[0], Ug[0]
                for j in range(1, 8):
                    us = jnp.where(subs == j, Us[j], us)
                    ug = jnp.where(subs == j, Ug[j], ug)
                parts = [jnp.concatenate([us, ug], 1)]
                if v0:
                    parts.insert(0, jnp.zeros((8 * v0, 2 * BLK), F32))
                parts.append(jnp.zeros((BLK - 8 * v0 - 8, 2 * BLK), F32))
                rank = split(jnp.concatenate(parts, 0))
                less = dot3(split(jnp.concatenate(S[far:], 0)), rank, NN)
                for v in range(far, 16):
                    at = slice(8 * (v - far), 8 * (v - far + 1))
                    S[v] = S[v] - less[at, :BLK]
                    G[v] = G[v] - less[at, BLK:]


def chol_inverse(A, W, Ls, T):
    pairs = A.shape[0] // 256
    W[...] = jnp.zeros(W.shape, F32)

    def step(kb, _):
        r0 = pl.multiple_of(kb * BLK, BLK)
        rows = [A[pl.ds(pl.multiple_of(r0 + 8 * v, 8), 8), pl.ds(r0, BLK)] for v in range(16)]
        factor_block(rows, W, r0, r0, T)

        @pl.when(kb % 2 == 0)
        def _():
            r1 = pl.multiple_of(r0 + BLK, BLK)
            low = dot3(split(A[pl.ds(r1, BLK), pl.ds(r0, BLK)]), split(W[pl.ds(r0, BLK), pl.ds(r0, BLK)]), NT)
            Ls[...] = low
            low = split(low)
            A[pl.ds(r1, BLK), pl.ds(r1, BLK)] -= dot3(low, low, NT)

        @pl.when(kb % 2 == 1)
        def _():
            q = pl.multiple_of(r0 - BLK, BLK)
            t = dot3(split(Ls[...]), split(W[pl.ds(q, BLK), pl.ds(q, BLK)]), NN)
            W[pl.ds(r0, BLK), pl.ds(q, BLK)] = -dot3(split(W[pl.ds(r0, BLK), pl.ds(r0, BLK)]), split(t), NN)

        for c in range(pairs):
            @pl.when(kb == 2 * c + 1)
            def _():
                lo, hi = 256 * c, 256 * (c + 1)
                wd = split(W[lo:hi, lo:hi])
                if c > 0:
                    W[lo:hi, :lo] = dot3(wd, split(W[lo:hi, :lo]), NN)
                if c < pairs - 1:
                    low = split(dot3(split(A[hi:, lo:hi]), wd, NT))
                    for n in range(c + 1, pairs):
                        a, b = 256 * n, 256 * (n + 1)
                        A[a:, a:b] -= dot3([x[a - hi :] for x in low], [x[a - hi : b - hi] for x in low], NT)
                    W[hi:, lo:hi] = -dot3(low, wd, NN)
                    if c > 0:
                        W[hi:, :lo] -= dot3(low, split(W[lo:hi, :lo]), NN)

        return 0

    lax.fori_loop(0, 2 * pairs, step, 0)


VMEM = pl.BlockSpec(memory_space=pltpu.VMEM)
PARAMS = pltpu.CompilerParams(vmem_limit_bytes=56 * 2**20)


def cost(flops, data):
    return pl.CostEstimate(flops=flops, bytes_accessed=data, transcendentals=0)


def position():
    tile = lax.axis_index("tile")
    return tile // 8, tile % 8


def times_inverse_t(x, w, put):
    for n in range(4):
        a, b = 256 * n, 256 * (n + 1)
        put(n, dot3((x[0][:, :b], x[1][:, :b]), (w[0][a:b, :b], w[1][a:b, :b]), NT))


def inverse_times(w, x, put):
    for n in range(4):
        a, b = 256 * n, 256 * (n + 1)
        put(n, dot3((w[0][a:b, :b], w[1][a:b, :b]), (x[0][:b], x[1][:b]), NN))


def store_split(hi, lo, index, x):
    h, l = split(x)
    hi[index] = h
    lo[index] = l


def block_at(index):
    return pl.ds(pl.multiple_of(index * BLK, BLK), BLK)


def finish_lower(whi, wlo, wa, low, wb):
    first, last = split(wa[...]), split(wb[...])
    below = split(-dot3(last, split(dot3(low, first, NN)), NN))
    for out, d0, d1, x in zip((whi, wlo), first, last, below):
        out[:512, :512] = d0
        out[:512, 512:] = jnp.zeros((512, 512), BF16)
        out[512:, :512] = x
        out[512:, 512:] = d1


def own_part(left, whi, wlo, index):
    return dot3(split(left), (whi[block_at(index), :], wlo[block_at(index), :]), NT)


def gather_first(pieces, row, col, A):
    for k in range(4):
        for n in range(4):
            A[block_at(((row ^ n) + 3) % 4), block_at((col % 4) ^ k)] = pieces[k][n * BLK : (n + 1) * BLK, :]


def kernel_a1(*refs):
    pieces = refs[:4]
    w, A, first, Ls, T = refs[4:]
    row, col = position()
    gather_first(pieces, row, col, A)
    first[...] = A[:256, :256]
    chol_inverse(first, w, Ls, T)


def kernel_a2(*refs):
    pieces = refs[:4]
    w, wa, top, A, last, wl, Ls, T = refs[4:]
    row, col = position()
    here = (row + 3) % 4
    gather_first(pieces, row, col, A)
    w11 = split(w[...])
    low = split(dot3(split(A[256:, :256]), w11, NT))
    last[...] = A[256:, 256:] - dot3(low, low, NT)
    chol_inverse(last, wl, Ls, T)
    wa[:256, :256] = w[...]
    wa[:256, 256:] = jnp.zeros((256, 256), F32)
    wa[256:, :256] = -dot3(split(wl[...]), split(dot3(low, w11, NN)), NN)
    wa[256:, 256:] = wl[...]
    own = dotp(A[block_at(here), :], wa[block_at(col % 4), :], NT)
    top[:, :BLK] = jnp.where((col < 4) & (here >= col), own, 0.0).astype(BF16)
    top[:, BLK:] = jnp.zeros((BLK, BLK), BF16)


def kernel_b(*refs):
    pieces = refs[:4]
    wa, whi, wlo, top, D, A, wb, lhi, llo, keep, Ls, T = refs[4:]
    row, col = position()
    here = (row + 3) % 4
    for k in range(4):
        for n in range(4):
            at = block_at(((row ^ n) + 3) % 4), block_at((col % 4) ^ k)
            D[at] = pieces[k][n * BLK : (n + 1) * BLK, :BLK]
            A[at] = pieces[k][n * BLK : (n + 1) * BLK, BLK:]
    keep[:, :512] = D[block_at(here), :]
    keep[:, 512:] = A[block_at(here), :]
    low = split(dot3(split(D[...]), split(wa[...]), NT))
    lhi[...], llo[...] = low
    A[...] -= dot3(low, low, NT)
    chol_inverse(A, wb, Ls, T)
    finish_lower(whi, wlo, wa, (lhi[...], llo[...]), wb)
    own = own_part(keep[...], whi, wlo, col)
    top[:, :BLK] = jnp.where(here + 4 >= col, own, 0.0).astype(BF16)
    top[:, BLK:] = jnp.zeros((BLK, BLK), BF16)


def place(src, i, x, xhi, xlo, blocks):
    rows = block_at(i)
    for half in range(2):
        store_split(xhi, xlo, (rows, block_at(4 * half + x)), src[:, half * BLK : (half + 1) * BLK])
    for n, ref in enumerate(blocks):
        ref[rows, block_at(x)] = src[:, (n + 2) * BLK : (n + 3) * BLK]


def spread(pieces, row, xhi, xlo, blocks):
    for k in range(4):
        for x in range(4):
            place(pieces[k][x], ((row ^ k) + 3) % 4, x, xhi, xlo, blocks)


def kernel_c(*refs):
    pieces = refs[:4]
    w0hi, w0lo, low, wc, top, A, xhi, xlo, keep, Ls, T = refs[4:]
    row, col = position()
    here = (row + 3) % 4
    for k in range(4):
        for n in range(4):
            place(pieces[k][n * BLK : (n + 1) * BLK, :], ((row ^ n) + 3) % 4, (col % 4) ^ k, xhi, xlo, [A])

    def put(n, x):
        low[:, 256 * n : 256 * (n + 1)] = x.astype(BF16)

    times_inverse_t((xhi, xlo), (w0hi, w0lo), put)
    A[...] -= dot(low[...], low[...], NT)
    keep[...] = A[block_at(here), :]
    chol_inverse(A, wc, Ls, T)
    own = dotp(keep[...], wc[block_at(col % 4), :], NT)
    top[:, :BLK] = low[block_at(here), block_at(col)]
    top[:, BLK:] = jnp.where((col < 4) & (here >= col), own, 0.0).astype(BF16)


def kernel_d(*refs):
    pieces = refs[:4]
    w0hi, w0lo, lowc, wc, low, whi, wlo, top, D, A, wd, lhi, llo, xhi, xlo, keep, Ls, T = refs[4:]
    row, col = position()
    here = (row + 3) % 4
    spread(pieces, row, xhi, xlo, [D, A])

    def put(n, x):
        low[:, 256 * n : 256 * (n + 1)] = x.astype(BF16)

    times_inverse_t((xhi, xlo), (w0hi, w0lo), put)
    D[...] -= dot(low[...], lowc[...], NT)
    A[...] -= dot(low[...], low[...], NT)
    keep[:, :512] = D[block_at(here), :]
    keep[:, 512:] = A[block_at(here), :]
    lower = split(dot3(split(D[...]), split(wc[...]), NT))
    lhi[...], llo[...] = lower
    A[...] -= dot3(lower, lower, NT)
    chol_inverse(A, wd, Ls, T)
    finish_lower(whi, wlo, wc, (lhi[...], llo[...]), wd)
    own = own_part(keep[...], whi, wlo, col)
    top[:, :BLK] = low[block_at(here), block_at(col)]
    top[:, BLK:] = jnp.where(here + 4 >= col, own, 0.0).astype(BF16)


def rows_kernel(panel, *refs):
    pieces, refs = refs[:4], refs[4:]
    row, col = position()
    if panel == 0:
        whi, wlo, out, x = refs
    else:
        whi, wlo, low_c, low_d, first, out, x = refs
    for k in range(4):
        for n in range(2):
            at = (2 * n + panel) * BLK
            x[:, block_at(col ^ k ^ (4 * n))] = pieces[k][:, at : at + BLK]
    v = x[...]
    if panel == 1:
        v = v - jnp.concatenate([dot(first[...].reshape(192, 1024), low[...], NT) for low in (low_c, low_d)], 1)

    def put(n, y):
        for h in range(2):
            out[h, :, 256 * n : 256 * (n + 1)] = y[96 * h : 96 * (h + 1)].astype(BF16)

    times_inverse_t(split(v), (whi, wlo), put)


def columns_first(*refs):
    top_z, top_y, low_y, low_z = refs[:4]
    w0hi, w0lo, low_c, low_d, t0, nhi, nlo, xhi, xlo, y = refs[4:]
    row, _ = position()
    for n in range(2):
        for top, side in ((top_z, row % 2), (top_y, 1 - row % 2)):
            at = (2 * n + side + 3) % 4
            for m in range(2):
                store_split(xhi, xlo, (block_at(4 * m + at), slice(None)), top[n, m * BLK : (m + 1) * BLK, :])
        for low, z in ((low_y, row // 2), (low_z, 1 - row // 2)):
            at = (2 * z + n + 3) % 4
            for m in range(2):
                y[block_at(4 * m + at), :] = low[n, m * BLK : (m + 1) * BLK, :]

    def put(n, v):
        t0[256 * n : 256 * (n + 1), :] = v.astype(BF16)

    inverse_times((w0hi, w0lo), (xhi, xlo), put)
    for n in range(2):
        at = slice(512 * n, 512 * (n + 1)), slice(None)
        store_split(nhi, nlo, at, y[at] - dot((low_c, low_d)[n][...], t0[...], NN))


def columns_second(nhi, nlo, whi, wlo, t1):
    def put(n, v):
        t1[256 * n : 256 * (n + 1), :] = v.astype(BF16)

    inverse_times((whi, wlo), (nhi, nlo), put)


def update_kernel(l0, *refs):
    pieces, (t0, t1, a0, a1, a2, out, factor, l1) = refs[:4], refs[4:]
    _, col = position()

    @pl.when(pl.program_id(0) == 0)
    def _():
        for k in range(4):
            for n in range(2):
                l1[pl.ds(pl.multiple_of((col ^ k ^ (4 * n)) * 96, 32), 96), :] = pieces[k][n]
        at = block_at(col)
        factor[:, :BLK] = l0[:, 0, :, at].reshape(768, BLK)
        factor[:, BLK:] = l1[:, at]

    total = dot(l0[:, 0].reshape(768, 1024), t0[...], NN) + dot(l1[...], t1[...], NN)
    for n, a in enumerate((a0, a1, a2)):
        at = slice(256 * n, 256 * (n + 1))
        out[at, :] = (a[...] - total[at]).astype(BF16)


def merge_kernel(owner, block_map, parent, *refs):
    children, (out, held, sem) = refs[:8], refs[8:]
    step = pl.program_id(0)
    me = lax.axis_index("front")
    row, col = position()
    here = (row + 3) % 4

    def copies(k):
        return [
            pltpu.make_async_copy(children[2 * k + h], held.at[k, pl.ds(768 * h, 768), :], sem.at[k, h])
            for h in range(2)
        ]

    for k in range(4):
        @pl.when((step == 0) & (owner[me ^ k] == me))
        def _():
            for copy in copies(k):
                copy.start()

    out[...] = parent[...].astype(F32)

    for k in range(4):
        @pl.when((step == 0) & (owner[me ^ k] == me))
        def _():
            for copy in copies(k):
                copy.wait()

    for k in range(4):
        @pl.when(owner[me ^ k] == me)
        def _():
            for b in range(6):
                j = block_map[me ^ k, 8 * b + col] >> 3

                @pl.when(j >> 1 == step)
                def _():
                    for a in range(12):
                        i = block_map[me ^ k, 4 * a + here] >> 2
                        x = held[k, a * BLK : (a + 1) * BLK, b * BLK : (b + 1) * BLK]
                        out[block_at(i), block_at(j & 1)] += x.astype(F32)


def per_device(fronts, parents, parent_of, block_map):
    tile = lax.axis_index("tile")
    row, col = tile // 8, tile % 8
    a = fronts[0, 0]
    big = jax.ShapeDtypeStruct((1024, 1024), BF16)
    mid = jax.ShapeDtypeStruct((512, 512), F32)
    wide = jax.ShapeDtypeStruct((512, 1024), BF16)
    top_shape = jax.ShapeDtypeStruct((BLK, 256), BF16)
    piece = pltpu.VMEM((512, 512), BF16)
    quarter = pltpu.VMEM((512, 512), F32)
    strip = pltpu.VMEM((512, 1024), BF16)
    line = pltpu.VMEM((BLK, 1024), F32)
    block = pltpu.VMEM((BLK, BLK), F32)
    rows_t = pltpu.VMEM((160, BLK), F32)

    crossing = jnp.sum(jnp.where(parent_of // 2 != jnp.arange(4) // 2, 1 << jnp.arange(4), 0))
    def swap(x, k):
        return lax.ppermute(x, "tile", [(i, i ^ k) for i in range(32)])

    def call(kernel, name, flops, ins, outs, scratch):
        return pl.pallas_call(
            kernel,
            out_shape=outs,
            in_specs=[VMEM] * len(ins),
            out_specs=(VMEM,) * len(outs),
            scratch_shapes=scratch,
            compiler_params=PARAMS,
            cost_estimate=cost(flops, 8_000_000),
            name=name,
        )(*ins)

    def core_swap(x):
        return lax.ppermute(x, "front", [(i, i ^ 1) for i in range(4)])

    def cross(x):
        def branch(mask):
            pairs = [(i, i ^ 2) for i in range(4) if mask >> i & 1]
            return lambda v: lax.ppermute(v, "front", pairs) if pairs else jnp.zeros_like(v)

        return lax.switch(crossing, [branch(mask) for mask in range(16)], x)

    x_groups = [[4 * y + x for x in range(4)] for y in range(8)]
    row_groups = [[8 * r + c for c in range(8)] for r in range(4)]
    y_groups = [[i, i + 8] for i in range(32) if not i & 8]
    z_groups = [[i, i + 16] for i in range(16)]
    low_half = col < 4

    def column_swap(x):
        return jnp.concatenate([x] + [swap(x, 8 * k) for k in range(1, 4)], 0)

    def x_swap(x):
        return [x] + [swap(x, k) for k in range(1, 4)]

    q0 = a[:BLK, :BLK]
    q0 = column_swap(jnp.where(low_half, q0, swap(q0, 4)))
    q0, rest = lax.optimization_barrier((q0, a[BLK:512, :256]))
    q0 = x_swap(q0)
    far = swap(rest, 4)
    lo = jnp.where(low_half, rest, far)
    hi = jnp.where(low_half, far, rest)
    q12 = jnp.concatenate(
        [lo[:BLK, :BLK], hi[:BLK, :BLK], lo[BLK : 2 * BLK, :BLK], hi[BLK : 2 * BLK, :BLK], lo[BLK : 2 * BLK, BLK:]], 1
    )
    q12 = column_swap(q12)
    q3 = jnp.concatenate([lo[2 * BLK :, :BLK], hi[2 * BLK :, :BLK], lo[2 * BLK :, BLK:], hi[2 * BLK :, BLK:]], 1)
    q3 = lax.all_gather(q3, "tile", axis=0, axis_index_groups=x_groups)
    trail = a[512:, :256].reshape(2, 2, 384, 256)
    half = col // 4
    near = lax.dynamic_index_in_dim(trail, half, 1, keepdims=False)
    away = lax.dynamic_index_in_dim(trail, 1 - half, 1, keepdims=False)
    side_top, side_low = a[:256, 256:], a[256:512, 256:]
    small = pltpu.VMEM((256, 256), F32)

    (w11,) = call(
        kernel_a1,
        "panel_a1",
        20_000_000_000,
        q0,
        (jax.ShapeDtypeStruct((256, 256), F32),),
        [quarter, small, block, rows_t],
    )
    w11, q12, away, side_top = lax.optimization_barrier((w11, q12, away, side_top))
    q1, q2 = x_swap(q12[:, : 2 * BLK]), q12[:, 2 * BLK :]
    far = swap(away, 4)
    side_top = lax.all_gather(side_top, "tile", axis=0, axis_index_groups=z_groups)
    wa, top0 = call(
        kernel_a2, "panel_a2", 20_000_000_000, q0 + [w11], (mid, top_shape), [quarter, small, small, block, rows_t]
    )
    wa, q2, q3, far, side_low, *q1 = lax.optimization_barrier((wa, q2, q3, far, side_low, *q1))
    low_y = lax.all_gather(side_low, "tile", axis=0, axis_index_groups=y_groups)
    q2 = x_swap(q2)
    q3_y, q3_z = swap(q3, 8), swap(q3, 16)
    w0hi, w0lo, top1 = call(
        kernel_b,
        "panel_b",
        32_000_000_000,
        q1 + [wa],
        (big, big, top_shape),
        [quarter, quarter, quarter, piece, piece, line, block, rows_t],
    )
    w0hi, far, q3_y, side_top, *q2 = lax.optimization_barrier((w0hi, far, q3_y, side_top, *q2))
    q3 = [q3, q3_y, q3_z, swap(q3_y, 16)]
    both = jnp.concatenate([near, far], 2).reshape(2, 4, 96, 512)
    pieces = [
        lax.dynamic_index_in_dim(both, (col % 4) ^ k, 1, keepdims=False).reshape(192, 512) for k in range(4)
    ]
    pieces = pieces[:1] + [swap(pieces[k], k) for k in range(1, 4)]
    top_y = swap(side_top, 8)
    low_c, wc, top2 = call(
        kernel_c,
        "panel_c",
        35_000_000_000,
        q2 + [w0hi, w0lo],
        (wide, mid, top_shape),
        [quarter, strip, strip, pltpu.VMEM((BLK, 512), F32), block, rows_t],
    )
    wc, top_y, low_y, *rest = lax.optimization_barrier((wc, top_y, low_y, *pieces, *q3))
    pieces, q3 = rest[:4], rest[4:]
    low_z = swap(low_y, 16)
    sub = jax.ShapeDtypeStruct((2, 96, 1024), BF16)
    (first,) = call(
        functools.partial(rows_kernel, 0),
        "first_rows",
        1_200_000_000,
        pieces + [w0hi, w0lo],
        (sub,),
        [pltpu.VMEM((192, 1024), F32)],
    )
    l0 = lax.all_gather(first, "tile", axis=0, axis_index_groups=row_groups)
    low_d, w1hi, w1lo, top3 = call(
        kernel_d,
        "panel_d",
        38_000_000_000,
        q3 + [w0hi, w0lo, low_c, wc],
        (wide, big, big, top_shape),
        [quarter, quarter, quarter, piece, piece, strip, strip, line, block, rows_t],
    )
    w1hi, low_z = lax.optimization_barrier((w1hi, low_z))
    (second,) = call(
        functools.partial(rows_kernel, 1),
        "second_rows",
        1_700_000_000,
        pieces + [w1hi, w1lo, low_c, low_d, first],
        (sub,),
        [pltpu.VMEM((192, 1024), F32)],
    )
    pair = swap(second, 4)
    tall = jax.ShapeDtypeStruct((1024, 768), BF16)
    second, side_top = lax.optimization_barrier((second, side_top))
    t0, nhi, nlo = call(
        columns_first,
        "columns_first",
        9_000_000_000,
        [side_top, top_y, low_y, low_z, w0hi, w0lo, low_c, low_d],
        (tall, tall, tall),
        [pltpu.VMEM((1024, 768), BF16)] * 2 + [pltpu.VMEM((1024, 768), F32)],
    )
    nhi, pair = lax.optimization_barrier((nhi, pair))
    later = jnp.stack([second[1], pair[1]])
    l1 = x_swap(jnp.stack([second[0], pair[0]]))
    (t1,) = call(
        columns_second, "columns_second", 9_000_000_000, [nhi, nlo, w1hi, w1lo], (tall,), []
    )
    l1 = [l1]

    def update(h):
        def rows_of(k):
            return pl.BlockSpec((256, 256), lambda j: (2 + 3 * h + k, 1 + j))

        return pl.pallas_call(
            update_kernel,
            grid=(3,),
            out_shape=(
                jax.ShapeDtypeStruct((768, 768), BF16),
                jax.ShapeDtypeStruct((768, 256), BF16),
            ),
            in_specs=[
                pl.BlockSpec((8, 1, 96, 1024), lambda j: (0, h, 0, 0)),
                *[pl.BlockSpec((2, 96, 1024), lambda j: (0, 0, 0))] * 4,
                pl.BlockSpec((1024, 256), lambda j: (0, j)),
                pl.BlockSpec((1024, 256), lambda j: (0, j)),
                rows_of(0),
                rows_of(1),
                rows_of(2),
            ],
            out_specs=(
                pl.BlockSpec((768, 256), lambda j: (0, j)),
                pl.BlockSpec((768, 256), lambda j: (0, 0)),
            ),
            scratch_shapes=[pltpu.VMEM((768, 1024), BF16)],
            compiler_params=PARAMS,
            cost_estimate=cost(2_500_000_000, 9_000_000),
            name="update",
        )(l0, *l1[h], t0, t1, a, a, a)

    children, lower = [], []
    for h in range(2):
        if h:
            across, *l1[1] = lax.optimization_barrier((across, *l1[1]))
            children[0] = (*children[0][:2], across, core_swap(across))
        own, below = update(h)
        if not h:
            own, later = lax.optimization_barrier((own, later))
            l1.append(x_swap(later))
        across = cross(own)
        children.append((own, core_swap(own), across, core_swap(across)))
        lower.append(below)
    factor = jnp.concatenate([top0, top1, top2, top3, *lower], 0)

    column = pl.BlockSpec((2048, 2 * BLK), lambda i, owner, block_map: (0, i))
    merged = pl.pallas_call(
        merge_kernel,
        grid_spec=pltpu.PrefetchScalarGridSpec(
            num_scalar_prefetch=2,
            grid=(4,),
            in_specs=[column] + [pl.BlockSpec(memory_space=pl.ANY)] * 8,
            out_specs=column,
            scratch_shapes=[pltpu.VMEM((4, 1536, 768), BF16), pltpu.SemaphoreType.DMA((4, 2))],
        ),
        out_shape=jax.ShapeDtypeStruct((2048, 1024), F32),
        compiler_params=PARAMS,
        cost_estimate=cost(10_000_000, 22_000_000),
        name="merge",
    )(parent_of, block_map, parents[0, 0], *[children[h][k] for k in range(4) for h in range(2)])
    return factor[None, None], merged[None, None]


def solution(mesh):
    return jax.shard_map(
        per_device,
        mesh=mesh,
        in_specs=(P("front", "tile", None, None), P("front", "tile", None, None), P(), P()),
        out_specs=(P("front", "tile", None, None), P("front", "tile", None, None)),
        check_vma=False,
    )
```

profile of v0, /device:TPU:16, one launch (start us, length us, event | category | flops | bytes accessed | tf_op | source)
XLA Modules:
  0.0 361.6 jit_solution(1593430843729100549)
XLA Ops:
  9.3 3.0 collective-permute-done.30
  15.5 2.7 collective-permute-start.33
  25.5 2.6 fusion.5
  29.6 2.7 collective-permute-start.35
  41.5 2.6 collective-permute-done.36.refs_3_
  44.8 9.5 %panel_a1.1.refs_4_ = f32[256,256]{1,0:T(8,128)} custom-call(f32[512,128]{1,0:T(8,128)} %copy-done.18, f32[512,128]{1,0:T(8,128)} %copy-done.29, f32[512,128]{1,0:T(8,128)} %copy-done.30, f32[512,128]{1,0:T(8,128)} %copy-done.31), custom_call_target="tpu_custom_call" | custom-call | flops 20000000000 | bytes 8000000 | tf_op jit(solution)/shard_map/panel_a1/pallas_call | solution.py:449
  56.5 2.8 collective-permute-start.44
  59.6 11.1 %panel_a2.1 = (f32[512,512]{1,0:T(8,128)}, bf16[128,256]{1,0:T(8,128)(2,1)}) custom-call(f32[512,128]{1,0:T(8,128)} %copy-done.18, f32[512,128]{1,0:T(8,128)} %copy-done.29, f32[512,128]{1,0:T(8,128)} %copy-done.30, f32[512,128]{1,0:T(8,128)} %copy-done.31, f32[256,256]{1,0:T(8,128)} %panel_a1.1.refs_4_), custom_call_target="tpu_custom_call" | custom-call | flops 20000000000 | bytes 8000000 | tf_op jit(solution)/shard_map/panel_a2/pallas_call | solution.py:449
  72.0 10.8 %collective-permute-done.43.refs_2_ = f32[512,256]{1,0:T(8,128)} collective-permute-done((f32[512,256]{1,0:T(8,128)S(1)}, f32[512,256]{1,0:T(8,128)}, u32[]{:S(2)}, u32[]{:S(2)}) %collective-permute-start.43) | collective-permute-done | bytes 524320 | tf_op jit(solution)/shard_map/ppermute | solution.py:446
  83.8 3.2 collective-permute-start.47
  90.0 24.2 %panel_b.1 = (bf16[1024,1024]{1,0:T(8,128)(2,1)}, bf16[1024,1024]{1,0:T(8,128)(2,1)}, bf16[128,256]{1,0:T(8,128)(2,1)}) custom-call(f32[512,256]{1,0:T(8,128)} %copy-done.10, f32[512,256]{1,0:T(8,128)} %collective-permute-done.42.refs_1_, f32[512,256]{1,0:T(8,128)} %collective-permute-done.43.refs_2_, f32[512,256]{1,0:T(8,128)} %collective-permute-done.44.refs_3_, ...), custom_call_target="tpu_custom_call" | custom-call | flops 32000000000 | bytes 8000000 | tf_op jit(solution)/shard_map/panel_b/pallas_call | solution.py:449
  114.2 6.1 %collective-permute-done.47.refs_2_ = f32[512,384]{1,0:T(8,128)S(1)} collective-permute-done((f32[512,384]{1,0:T(8,128)S(1)}, f32[512,384]{1,0:T(8,128)S(1)}, u32[]{:S(2)}, u32[]{:S(2)}) %collective-permute-start.47) | collective-permute-done | bytes 786464 | tf_op jit(solution)/shard_map/ppermute | solution.py:446
  120.3 2.7 collective-permute-done.48.refs_3_
  132.3 24.5 %panel_c.1 = (bf16[512,1024]{1,0:T(8,128)(2,1)}, f32[512,512]{1,0:T(8,128)}, bf16[128,256]{1,0:T(8,128)(2,1)}) custom-call(f32[512,384]{1,0:T(8,128)} %copy-done.9, f32[512,384]{1,0:T(8,128)} %copy-done.27, f32[512,384]{1,0:T(8,128)} %copy-done.28, f32[512,384]{1,0:T(8,128)} %collective-permute-done.48.refs_3_, ...), custom_call_target="tpu_custom_call" | custom-call | flops 35000000512 | bytes 8000000 | tf_op jit(solution)/shard_map/panel_c/pallas_call | solution.py:449
  156.9 14.9 %collective-permute-done.49.refs_1_ = f32[2,256,768]{2,1,0:T(8,128)} collective-permute-done((f32[2,256,768]{2,1,0:T(8,128)S(1)}, f32[2,256,768]{2,1,0:T(8,128)}, u32[]{:S(2)}, u32[]{:S(2)}) %collective-permute-start.49) | collective-permute-done | bytes 1572896 | tf_op jit(solution)/shard_map/ppermute | solution.py:446
  174.1 5.0 %first_rows.1.refs_8_ = bf16[2,96,1024]{2,1,0:T(8,128)(2,1)} custom-call(f32[192,512]{1,0:T(8,128)} %bitcast.35, f32[192,512]{1,0:T(8,128)} %copy-done.2, f32[192,512]{1,0:T(8,128)} %copy-done.3, f32[192,512]{1,0:T(8,128)} %copy-done.4, bf16[1024,1024]{1,0:T(8,128)(2,1)} %get-tuple-element.154.refs_4_, bf16[1024,1024]{1,0:T(8,128)(2,1)} %get-tuple-element.155.refs_5_), custom_call_target="tpu_custom_call" | custom-call | flops 1200000000 | bytes 8000000 | tf_op jit(solution)/shard_map/first_rows/pallas_call | solution.py:449
  179.1 30.6 %panel_d.1 = (bf16[512,1024]{1,0:T(8,128)(2,1)}, bf16[1024,1024]{1,0:T(8,128)(2,1)}, bf16[1024,1024]{1,0:T(8,128)(2,1)}, bf16[128,256]{1,0:T(8,128)(2,1)}) custom-call(f32[4,128,512]{2,1,0:T(8,128)} %bitcast.48, f32[4,128,512]{2,1,0:T(8,128)} %collective-permute-done.45.refs_1_, f32[4,128,512]{2,1,0:T(8,128)} %collective-permute-done.53.refs_2_, ...), custom_call_target="tpu_custom_call" | custom-call | flops 38000001024 | bytes 8000000 | tf_op jit(solution)/shard_map/panel_d/pallas_call | solution.py:449
  209.6 6.8 %second_rows.1 = bf16[2,96,1024]{2,1,0:T(8,128)(2,1)} custom-call(f32[192,512]{1,0:T(8,128)} %bitcast.36, f32[192,512]{1,0:T(8,128)} %copy-done.2, f32[192,512]{1,0:T(8,128)} %copy-done.3, f32[192,512]{1,0:T(8,128)} %copy-done.4, bf16[1024,1024]{1,0:T(8,128)(2,1)} %get-tuple-element.175.refs_4_.whi, bf16[1024,1024]{1,0:T(8,128)(2,1)} %get-tuple-element.176.refs_5_.wlo, ...), custom_call_target="tpu_custom_call" | custom-call | flops 1700000000 | bytes 8000000 | tf_op jit(solution)/shard_map/second_rows/pallas_call | solution.py:449
  218.7 12.0 %columns_first.1 = (bf16[1024,768]{1,0:T(8,128)(2,1)}, bf16[1024,768]{1,0:T(8,128)(2,1)}, bf16[1024,768]{1,0:T(8,128)(2,1)}) custom-call(f32[2,256,768]{2,1,0:T(8,128)} %bitcast.42, f32[2,256,768]{2,1,0:T(8,128)} %collective-permute-done.49.refs_1_, f32[2,256,768]{2,1,0:T(8,128)} %bitcast.45, f32[2,256,768]{2,1,0:T(8,128)} %copy-done.26, ...), custom_call_target="tpu_custom_call" | custom-call | flops 8999999488 | bytes 8000000 | tf_op jit(solution)/shard_map/columns_first/pallas_call | solution.py:449
  232.3 2.7 collective-permute-start.58
  236.0 7.5 %columns_second.1.refs_5_ = bf16[1024,768]{1,0:T(8,128)(2,1)} custom-call(bf16[1024,768]{1,0:T(8,128)(2,1)} %get-tuple-element.185.nhi, bf16[1024,768]{1,0:T(8,128)(2,1)} %get-tuple-element.186.nlo, bf16[1024,1024]{1,0:T(8,128)(2,1)} %get-tuple-element.175.refs_4_.whi, bf16[1024,1024]{1,0:T(8,128)(2,1)} %get-tuple-element.176.refs_5_.wlo), custom_call_target="tpu_custom_call" | custom-call | flops 8999999488 | bytes 8000000 | tf_op jit(solution)/shard_map/columns_second/pallas_call | solution.py:449
  243.6 8.8 %collective-permute-done.58.refs_2_ = bf16[2,96,1024]{2,1,0:T(8,128)(2,1)S(1)} collective-permute-done((bf16[2,96,1024]{2,1,0:T(8,128)(2,1)S(1)}, bf16[2,96,1024]{2,1,0:T(8,128)(2,1)S(1)}, u32[]{:S(2)}, u32[]{:S(2)}) %collective-permute-start.58) | collective-permute-done | bytes 393248 | tf_op jit(solution)/shard_map/ppermute | solution.py:446
  255.7 6.8 %update.2 = (bf16[768,768]{1,0:T(8,128)(2,1)S(1)}, bf16[768,256]{1,0:T(8,128)(2,1)}) custom-call(bf16[8,2,96,1024]{3,2,1,0:T(8,128)(2,1)} %bitcast.30, bf16[2,96,1024]{2,1,0:T(8,128)(2,1)} %copy-done.1, bf16[2,96,1024]{2,1,0:T(8,128)(2,1)} %copy-done.13, bf16[2,96,1024]{2,1,0:T(8,128)(2,1)} %copy-done.14, bf16[2,96,1024]{2,1,0:T(8,128)(2,1)} %copy-done.15, ...), custom_call_target="tpu_custom_call" | custom-call | flops 2500000000 | bytes 9000000 | tf_op jit(solution)/shard_map/update/pallas_call | solution.py:598
  262.5 2.6 collective-permute-start.61
  268.6 31.2 %conditional.2 = (bf16[768,768]{1,0:T(8,128)(2,1)}) conditional(s32[]{:T(128)} %clamp.4, () %tuple.122, bf16[768,768]{1,0:T(8,128)(2,1)S(1)} %get-tuple-element.189.refs_0_, bf16[768,768]{1,0:T(8,128)(2,1)S(1)} %get-tuple-element.189.refs_0_, bf16[768,768]{1,0:T(8,128)(2,1)S(1)} %get-tuple-element.189.refs_0_, ...), branch_computations={%region_1.2_spmd, %region_2.3_spmd, %region_3.4_spmd, %region_4.5_... | conditional | bytes 4718640 | solution.py:468
  268.6 5.1 %collective-permute-start.6 = (bf16[768,768]{1,0:T(8,128)(2,1)S(1)}, bf16[768,768]{1,0:T(8,128)(2,1)}, u32[]{:S(2)}, u32[]{:S(2)}) collective-permute-start(bf16[768,768]{1,0:T(8,128)(2,1)S(1)} %param.7), channel_id=1, source_target_pairs={{0,64},{32,96},{64,0},{1,65},{33,97},{65,1},{2,66},{34,98},{66,2},... | collective-permute-start | bytes 3538952 | tf_op jit(solution)/shard_map/cond/branch_7_fun/ppermute | solution.py:466
  273.7 25.8 %collective-permute-done.6 = bf16[768,768]{1,0:T(8,128)(2,1)} collective-permute-done((bf16[768,768]{1,0:T(8,128)(2,1)S(1)}, bf16[768,768]{1,0:T(8,128)(2,1)}, u32[]{:S(2)}, u32[]{:S(2)}) %collective-permute-start.6) | collective-permute-done | bytes 1179680 | tf_op jit(solution)/shard_map/cond/branch_7_fun/ppermute | solution.py:466
  300.7 7.0 %update.3 = (bf16[768,768]{1,0:T(8,128)(2,1)}, bf16[768,256]{1,0:T(8,128)(2,1)}) custom-call(bf16[8,2,96,1024]{3,2,1,0:T(8,128)(2,1)} %bitcast.31, bf16[2,96,1024]{2,1,0:T(8,128)(2,1)} %copy-done, bf16[2,96,1024]{2,1,0:T(8,128)(2,1)} %copy-done.11, bf16[2,96,1024]{2,1,0:T(8,128)(2,1)} %copy-done.12, bf16[2,96,1024]{2,1,0:T(8,128)(2,1)} %collective-permute-done.62.refs_3_, ...), custom_call_target="tpu_custom_call" | custom-call | flops 2500000000 | bytes 9000000 | tf_op jit(solution)/shard_map/update/pallas_call | solution.py:598
  307.9 32.2 %conditional.3 = (bf16[768,768]{1,0:T(8,128)(2,1)}) conditional(s32[]{:T(128)} %clamp.4, () %tuple.125, bf16[768,768]{1,0:T(8,128)(2,1)} %get-tuple-element.196.refs_1_, bf16[768,768]{1,0:T(8,128)(2,1)} %get-tuple-element.196.refs_1_, bf16[768,768]{1,0:T(8,128)(2,1)} %get-tuple-element.196.refs_1_, ...), branch_computations={%region_17.18_spmd, %region_18.19_spmd, %region_19.20_spmd, %regio... | conditional | bytes 4718640 | solution.py:468
  307.9 6.1 %collective-permute-start.21 = (bf16[768,768]{1,0:T(8,128)(2,1)}, bf16[768,768]{1,0:T(8,128)(2,1)}, u32[]{:S(2)}, u32[]{:S(2)}) collective-permute-start(bf16[768,768]{1,0:T(8,128)(2,1)} %param.23), channel_id=1, source_target_pairs={{0,64},{32,96},{64,0},{1,65},{33,97},{65,1},{2,66},{34,98},{66,2},... | collective-permute-start | bytes 3538952 | tf_op jit(solution)/shard_map/cond/branch_7_fun/ppermute | solution.py:466
  314.1 26.0 %collective-permute-done.21 = bf16[768,768]{1,0:T(8,128)(2,1)} collective-permute-done((bf16[768,768]{1,0:T(8,128)(2,1)}, bf16[768,768]{1,0:T(8,128)(2,1)}, u32[]{:S(2)}, u32[]{:S(2)}) %collective-permute-start.21) | collective-permute-done | bytes 1179680 | tf_op jit(solution)/shard_map/cond/branch_7_fun/ppermute | solution.py:466
  345.8 8.8 %merge.1 = f32[2048,1024]{1,0:T(8,128)} custom-call(s32[4]{0:T(128)} %owner.1, s32[4,48]{1,0:T(4,128)} %block_map.1, bf16[2048,1024]{1,0:T(8,128)(2,1)} %bitcast.34, bf16[768,768]{1,0:T(8,128)(2,1)S(1)} %get-tuple-element.189.refs_0_, bf16[768,768]{1,0:T(8,128)(2,1)} %get-tuple-element.196.refs_1_, bf16[768,768]{1,0:T(8,128)(2,1)} %copy-done.6, ...), custom_call_target="tpu_custom_call" | custom-call | flops 10000000 | bytes 22000000 | tf_op jit(solution)/shard_map/merge/pallas_call | solution.py:639
  (164 shorter events, 60.9 us)
Async XLA Ops:
  7.2 75.7 %all-gather.9.cloned.1.call-start = ((), (), s32[]{:S(2)}) async-start(), calls=%async_computation | async-start | bytes 1310720 | tf_op jit(solution)/shard_map/all_gather | solution.py:494
  33.0 21.3 %collective-permute-start.38 = (f32[128,640]{1,0:T(8,128)S(1)}, f32[128,640]{1,0:T(8,128)S(1)}, u32[]{:S(2)}, u32[]{:S(2)}) collective-permute-start(f32[128,640]{1,0:T(8,128)S(1)} %get-tuple-element.214), channel_id=1, source_target_pairs={{0,8},{1,9},{2,10},{3,11},{4,12},{5,13},{6,14},{7,15},{8,0},{9,1},... | collective-permute-start | bytes 983048 | tf_op jit(solution)/shard_map/ppermute | solution.py:446
  35.1 19.1 %collective-permute-start.39 = (f32[128,640]{1,0:T(8,128)S(1)}, f32[128,640]{1,0:T(8,128)S(1)}, u32[]{:S(2)}, u32[]{:S(2)}) collective-permute-start(f32[128,640]{1,0:T(8,128)S(1)} %get-tuple-element.214), channel_id=1, source_target_pairs={{0,16},{1,17},{2,18},{3,19},{4,20},{5,21},{6,22},{7,23},{8,24},{9,... | collective-permute-start | bytes 983048 | tf_op jit(solution)/shard_map/ppermute | solution.py:446
  35.9 78.3 %all-gather.11.cloned.1.call-start = ((), (), s32[]{:S(2)}) async-start(), calls=%async_computation.1 | async-start | bytes 2359296 | tf_op jit(solution)/shard_map/all_gather | solution.py:513
  36.4 17.9 %collective-permute-start.40 = (f32[128,640]{1,0:T(8,128)S(1)}, f32[128,640]{1,0:T(8,128)S(1)}, u32[]{:S(2)}, u32[]{:S(2)}) collective-permute-start(f32[128,640]{1,0:T(8,128)S(1)} %get-tuple-element.214), channel_id=1, source_target_pairs={{0,24},{1,25},{2,26},{3,27},{4,28},{5,29},{6,30},{7,31},{8,16},{9,... | collective-permute-start | bytes 983048 | tf_op jit(solution)/shard_map/ppermute | solution.py:446
  54.4 17.5 %collective-permute-start.42 = (f32[512,256]{1,0:T(8,128)S(1)}, f32[512,256]{1,0:T(8,128)}, u32[]{:S(2)}, u32[]{:S(2)}) collective-permute-start(f32[512,256]{1,0:T(8,128)S(1)} %slice.75.refs_0_), channel_id=1, source_target_pairs={{0,1},{1,0},{2,3},{3,2},{4,5},{5,4},{6,7},{7,6},{8,9},{9,8},{10,11... | collective-permute-start | bytes 1572872 | tf_op jit(solution)/shard_map/ppermute | solution.py:446
  54.5 28.3 %collective-permute-start.43 = (f32[512,256]{1,0:T(8,128)S(1)}, f32[512,256]{1,0:T(8,128)}, u32[]{:S(2)}, u32[]{:S(2)}) collective-permute-start(f32[512,256]{1,0:T(8,128)S(1)} %slice.75.refs_0_), channel_id=1, source_target_pairs={{0,2},{1,3},{2,0},{3,1},{4,6},{5,7},{6,4},{7,5},{8,10},{9,11},{10,... | collective-permute-start | bytes 1572872 | tf_op jit(solution)/shard_map/ppermute | solution.py:446
  56.5 26.4 %collective-permute-start.44 = (f32[512,256]{1,0:T(8,128)S(1)}, f32[512,256]{1,0:T(8,128)}, u32[]{:S(2)}, u32[]{:S(2)}) collective-permute-start(f32[512,256]{1,0:T(8,128)S(1)} %slice.75.refs_0_), channel_id=1, source_target_pairs={{0,3},{1,2},{2,1},{3,0},{4,7},{5,6},{6,5},{7,4},{8,11},{9,10},{10,... | collective-permute-start | bytes 1572872 | tf_op jit(solution)/shard_map/ppermute | solution.py:446
  59.2 23.6 %collective-permute-start.41 = (f32[2,384,256]{2,1,0:T(8,128)}, f32[2,384,256]{2,1,0:T(8,128)}, u32[]{:S(2)}, u32[]{:S(2)}) collective-permute-start(f32[2,384,256]{2,1,0:T(8,128)} %get-tuple-element.138), channel_id=1, source_target_pairs={{0,4},{1,5},{2,6},{3,7},{4,0},{5,1},{6,2},{7,3},{8,12},{9,13},{10,... | collective-permute-start | bytes 2359304 | tf_op jit(solution)/shard_map/ppermute | solution.py:446
  59.5 97.4 %all-gather.13.cloned.1.call-start = ((), (), s32[]{:S(2)}) async-start(), calls=%async_computation.2 | async-start | bytes 2359296 | tf_op jit(solution)/shard_map/all_gather | solution.py:518
  82.8 31.4 %collective-permute-start.46 = (f32[512,384]{1,0:T(8,128)S(1)}, f32[512,384]{1,0:T(8,128)S(1)}, u32[]{:S(2)}, u32[]{:S(2)}) collective-permute-start(f32[512,384]{1,0:T(8,128)S(1)} %slice.69.refs_0_), channel_id=1, source_target_pairs={{0,1},{1,0},{2,3},{3,2},{4,5},{5,4},{6,7},{7,6},{8,9},{9,8},{10,11... | collective-permute-start | bytes 2359304 | tf_op jit(solution)/shard_map/ppermute | solution.py:446
  83.8 36.5 %collective-permute-start.47 = (f32[512,384]{1,0:T(8,128)S(1)}, f32[512,384]{1,0:T(8,128)S(1)}, u32[]{:S(2)}, u32[]{:S(2)}) collective-permute-start(f32[512,384]{1,0:T(8,128)S(1)} %slice.69.refs_0_), channel_id=1, source_target_pairs={{0,2},{1,3},{2,0},{3,1},{4,6},{5,7},{6,4},{7,5},{8,10},{9,11},{10,... | collective-permute-start | bytes 2359304 | tf_op jit(solution)/shard_map/ppermute | solution.py:446
  87.0 36.0 %collective-permute-start.48 = (f32[512,384]{1,0:T(8,128)S(1)}, f32[512,384]{1,0:T(8,128)}, u32[]{:S(2)}, u32[]{:S(2)}) collective-permute-start(f32[512,384]{1,0:T(8,128)S(1)} %slice.69.refs_0_), channel_id=1, source_target_pairs={{0,3},{1,2},{2,1},{3,0},{4,7},{5,6},{6,5},{7,4},{8,11},{9,10},{10,... | collective-permute-start | bytes 2359304 | tf_op jit(solution)/shard_map/ppermute | solution.py:446
  87.8 35.2 %collective-permute-start.45 = (f32[4,128,512]{2,1,0:T(8,128)}, f32[4,128,512]{2,1,0:T(8,128)}, u32[]{:S(2)}, u32[]{:S(2)}) collective-permute-start(f32[4,128,512]{2,1,0:T(8,128)} %bitcast.46), channel_id=1, source_target_pairs={{0,8},{1,9},{2,10},{3,11},{4,12},{5,13},{6,14},{7,15},{8,0},{9,1},... | collective-permute-start | bytes 3145736 | tf_op jit(solution)/shard_map/ppermute | solution.py:446
  88.3 41.9 %collective-permute-start.53 = (f32[4,128,512]{2,1,0:T(8,128)}, f32[4,128,512]{2,1,0:T(8,128)}, u32[]{:S(2)}, u32[]{:S(2)}) collective-permute-start(f32[4,128,512]{2,1,0:T(8,128)} %bitcast.47), channel_id=1, source_target_pairs={{0,16},{1,17},{2,18},{3,19},{4,20},{5,21},{6,22},{7,23},{8,24},{9,... | collective-permute-start | bytes 3145736 | tf_op jit(solution)/shard_map/ppermute | solution.py:446
  90.0 165.0 %all-gather.15.cloned.1.call-start = ((), (), s32[]{:S(2)}) async-start(), calls=%async_computation.3 | async-start | bytes 3538944 | tf_op jit(solution)/shard_map/all_gather | solution.py:557
  125.3 31.5 %collective-permute-start.50 = (f32[192,512]{1,0:T(8,128)S(1)}, f32[192,512]{1,0:T(8,128)S(1)}, u32[]{:S(2)}, u32[]{:S(2)}) collective-permute-start(f32[192,512]{1,0:T(8,128)S(1)} %bitcast.40), channel_id=1, source_target_pairs={{0,1},{1,0},{2,3},{3,2},{4,5},{5,4},{6,7},{7,6},{8,9},{9,8},{10,11... | collective-permute-start | bytes 1179656 | tf_op jit(solution)/shard_map/ppermute | solution.py:446
  125.3 31.5 %collective-permute-start.51 = (f32[192,512]{1,0:T(8,128)S(1)}, f32[192,512]{1,0:T(8,128)S(1)}, u32[]{:S(2)}, u32[]{:S(2)}) collective-permute-start(f32[192,512]{1,0:T(8,128)S(1)} %bitcast.39), channel_id=1, source_target_pairs={{0,2},{1,3},{2,0},{3,1},{4,6},{5,7},{6,4},{7,5},{8,10},{9,11},{10,... | collective-permute-start | bytes 1179656 | tf_op jit(solution)/shard_map/ppermute | solution.py:446
  127.8 29.0 %collective-permute-start.52 = (f32[192,512]{1,0:T(8,128)S(1)}, f32[192,512]{1,0:T(8,128)S(1)}, u32[]{:S(2)}, u32[]{:S(2)}) collective-permute-start(f32[192,512]{1,0:T(8,128)S(1)} %bitcast.38), channel_id=1, source_target_pairs={{0,3},{1,2},{2,1},{3,0},{4,7},{5,6},{6,5},{7,4},{8,11},{9,10},{10,... | collective-permute-start | bytes 1179656 | tf_op jit(solution)/shard_map/ppermute | solution.py:446
  130.0 41.8 %collective-permute-start.49 = (f32[2,256,768]{2,1,0:T(8,128)S(1)}, f32[2,256,768]{2,1,0:T(8,128)}, u32[]{:S(2)}, u32[]{:S(2)}) collective-permute-start(f32[2,256,768]{2,1,0:T(8,128)S(1)} %bitcast.43), channel_id=1, source_target_pairs={{0,8},{1,9},{2,10},{3,11},{4,12},{5,13},{6,14},{7,15},{8,0},{9,1},... | collective-permute-start | bytes 4718600 | tf_op jit(solution)/shard_map/ppermute | solution.py:446
  130.3 26.7 %collective-permute-start.54 = (f32[4,128,512]{2,1,0:T(8,128)}, f32[4,128,512]{2,1,0:T(8,128)}, u32[]{:S(2)}, u32[]{:S(2)}) collective-permute-start(f32[4,128,512]{2,1,0:T(8,128)} %collective-permute-done.45.refs_1_), channel_id=1, source_target_pairs={{0,16},{1,17},{2,18},{3,19},{4,20},{5,21},{6,22},{7,23},{8,24},{9,... | collective-permute-start | bytes 3145736 | tf_op jit(solution)/shard_map/ppermute | solution.py:446
  171.8 37.8 %collective-permute-start.55 = (f32[2,256,768]{2,1,0:T(8,128)}, f32[2,256,768]{2,1,0:T(8,128)S(1)}, u32[]{:S(2)}, u32[]{:S(2)}) collective-permute-start(f32[2,256,768]{2,1,0:T(8,128)} %bitcast.44), channel_id=1, source_target_pairs={{0,16},{1,17},{2,18},{3,19},{4,20},{5,21},{6,22},{7,23},{8,24},{9,... | collective-permute-start | bytes 4718600 | tf_op jit(solution)/shard_map/ppermute | solution.py:446
  216.4 14.7 %collective-permute-start.56 = (bf16[2,96,1024]{2,1,0:T(8,128)(2,1)}, bf16[2,96,1024]{2,1,0:T(8,128)(2,1)S(1)}, u32[]{:S(2)}, u32[]{:S(2)}) collective-permute-start(bf16[2,96,1024]{2,1,0:T(8,128)(2,1)} %second_rows.1), channel_id=1, source_target_pairs={{0,4},{1,5},{2,6},{3,7},{4,0},{5,1},{6,2},{7,3},{8,12},{9,13},{10,... | collective-permute-start | bytes 1179656 | tf_op jit(solution)/shard_map/ppermute | solution.py:446
  232.3 20.0 %collective-permute-start.58 = (bf16[2,96,1024]{2,1,0:T(8,128)(2,1)S(1)}, bf16[2,96,1024]{2,1,0:T(8,128)(2,1)S(1)}, u32[]{:S(2)}, u32[]{:S(2)}) collective-permute-start(bf16[2,96,1024]{2,1,0:T(8,128)(2,1)S(1)} %pad_maximum_fusion.1.refs_0_), channel_id=1, source_target_pairs={{0,2},{1,3},{2,0},{3,1},{4,6},{5,7},{6,4},{7,5},{8,10},{9,11},{10,... | collective-permute-start | bytes 1179656 | tf_op jit(solution)/shard_map/ppermute | solution.py:446
  235.0 19.9 %collective-permute-start.59 = (bf16[2,96,1024]{2,1,0:T(8,128)(2,1)S(1)}, bf16[2,96,1024]{2,1,0:T(8,128)(2,1)S(1)}, u32[]{:S(2)}, u32[]{:S(2)}) collective-permute-start(bf16[2,96,1024]{2,1,0:T(8,128)(2,1)S(1)} %pad_maximum_fusion.1.refs_0_), channel_id=1, source_target_pairs={{0,3},{1,2},{2,1},{3,0},{4,7},{5,6},{6,5},{7,4},{8,11},{9,10},{10,... | collective-permute-start | bytes 1179656 | tf_op jit(solution)/shard_map/ppermute | solution.py:446
  262.5 37.3 %collective-permute-start.60 = (bf16[2,96,1024]{2,1,0:T(8,128)(2,1)S(1)}, bf16[2,96,1024]{2,1,0:T(8,128)(2,1)S(1)}, u32[]{:S(2)}, u32[]{:S(2)}) collective-permute-start(bf16[2,96,1024]{2,1,0:T(8,128)(2,1)S(1)} %pad_maximum_fusion.2.refs_0_), channel_id=1, source_target_pairs={{0,1},{1,0},{2,3},{3,2},{4,5},{5,4},{6,7},{7,6},{8,9},{9,8},{10,11... | collective-permute-start | bytes 1179656 | tf_op jit(solution)/shard_map/ppermute | solution.py:446
  262.5 37.3 %collective-permute-start.61 = (bf16[2,96,1024]{2,1,0:T(8,128)(2,1)S(1)}, bf16[2,96,1024]{2,1,0:T(8,128)(2,1)S(1)}, u32[]{:S(2)}, u32[]{:S(2)}) collective-permute-start(bf16[2,96,1024]{2,1,0:T(8,128)(2,1)S(1)} %pad_maximum_fusion.2.refs_0_), channel_id=1, source_target_pairs={{0,2},{1,3},{2,0},{3,1},{4,6},{5,7},{6,4},{7,5},{8,10},{9,11},{10,... | collective-permute-start | bytes 1179656 | tf_op jit(solution)/shard_map/ppermute | solution.py:446
  265.1 34.7 %collective-permute-start.62 = (bf16[2,96,1024]{2,1,0:T(8,128)(2,1)S(1)}, bf16[2,96,1024]{2,1,0:T(8,128)(2,1)}, u32[]{:S(2)}, u32[]{:S(2)}) collective-permute-start(bf16[2,96,1024]{2,1,0:T(8,128)(2,1)S(1)} %pad_maximum_fusion.2.refs_0_), channel_id=1, source_target_pairs={{0,3},{1,2},{2,1},{3,0},{4,7},{5,6},{6,5},{7,4},{8,11},{9,10},{10,... | collective-permute-start | bytes 1179656 | tf_op jit(solution)/shard_map/ppermute | solution.py:446
  268.5 72.2 %collective-permute-start.63 = (bf16[768,768]{1,0:T(8,128)(2,1)S(1)}, bf16[768,768]{1,0:T(8,128)(2,1)S(1)}, u32[]{:S(2)}, u32[]{:S(2)}) collective-permute-start(bf16[768,768]{1,0:T(8,128)(2,1)S(1)} %get-tuple-element.189.refs_0_), channel_id=1, source_target_pairs={{0,32},{32,0},{64,96},{96,64},{1,33},{33,1},{65,97},{97,65},{2,34}... | collective-permute-start | bytes 3538952 | tf_op jit(solution)/shard_map/ppermute | solution.py:461
  268.6 30.9 %collective-permute-start.6 = (bf16[768,768]{1,0:T(8,128)(2,1)S(1)}, bf16[768,768]{1,0:T(8,128)(2,1)}, u32[]{:S(2)}, u32[]{:S(2)}) collective-permute-start(bf16[768,768]{1,0:T(8,128)(2,1)S(1)} %param.7), channel_id=1, source_target_pairs={{0,64},{32,96},{64,0},{1,65},{33,97},{65,1},{2,66},{34,98},{66,2},... | collective-permute-start | bytes 3538952 | tf_op jit(solution)/shard_map/cond/branch_7_fun/ppermute | solution.py:466
  307.8 35.3 %collective-permute-start.64 = (bf16[768,768]{1,0:T(8,128)(2,1)}, bf16[768,768]{1,0:T(8,128)(2,1)}, u32[]{:S(2)}, u32[]{:S(2)}) collective-permute-start(bf16[768,768]{1,0:T(8,128)(2,1)} %get-tuple-element.196.refs_1_), channel_id=1, source_target_pairs={{0,32},{32,0},{64,96},{96,64},{1,33},{33,1},{65,97},{97,65},{2,34}... | collective-permute-start | bytes 3538952 | tf_op jit(solution)/shard_map/ppermute | solution.py:461
  307.9 32.1 %collective-permute-start.21 = (bf16[768,768]{1,0:T(8,128)(2,1)}, bf16[768,768]{1,0:T(8,128)(2,1)}, u32[]{:S(2)}, u32[]{:S(2)}) collective-permute-start(bf16[768,768]{1,0:T(8,128)(2,1)} %param.23), channel_id=1, source_target_pairs={{0,64},{32,96},{64,0},{1,65},{33,97},{65,1},{2,66},{34,98},{66,2},... | collective-permute-start | bytes 3538952 | tf_op jit(solution)/shard_map/cond/branch_7_fun/ppermute | solution.py:466
  (43 other events, 543.1 us)
Sparse Core Ops, SparseCore 0:
  36.0 28.4 all-gather.8
  66.1 39.6 all-gather.10
  107.5 39.7 all-gather.12
  179.2 45.5 all-gather.14
where the time goes:
time: 360 us; the launch traced here: 362 us
  Pallas kernels  154 us (43%)
  waiting for transfers between devices  113 us (31%)
  starting transfers between devices  63.2 us (18%)
  between operations  15.5 us (4%)
  local copies, waits for them, and re-layouts  10.8 us (3%)
  other arithmetic  4.75 us (1%)
    pallas_call x9, Pallas kernels, call(): pl.pallas_call(kernel, out_shape=outs, in_specs=[VMEM] * len(ins), out_sp...  131 us
    ppermute x33, waiting for transfers between devices, swap(): return lax.ppermute(x, 'tile', [(i, i ^ k) for i in range(32)])  57.4 us
    ppermute x2, waiting for transfers between devices, branch(): lax.ppermute(v, 'front', pairs)  51.8 us
    ppermute x33, starting transfers between devices, swap(): return lax.ppermute(x, 'tile', [(i, i ^ k) for i in range(32)])  51.2 us
    pallas_call x2, Pallas kernels, update(): pl.pallas_call(update_kernel, grid=(3,), out_shape=(jax.ShapeDtypeStruct(...  13.9 us
    ppermute x2, starting transfers between devices, branch(): lax.ppermute(v, 'front', pairs)  11.2 us
    pallas_call x1, Pallas kernels, per_device(): pl.pallas_call(merge_kernel, grid_spec=pltpu.PrefetchScalarGridSpec(num_s...  8.8 us
  transfers between devices with their start and end apart: 43, of which 17 were waited for; matrix products, arithmetic and copies ran while one was open for 3% of the time, Pallas kernels for 38%

commit v1 on v0

--- a/solution.py
+++ b/solution.py
@@ -337,18 +337,19 @@
 
 
 def columns_first(*refs):
-    top_z, top_y, low_y, low_z = refs[:4]
-    w0hi, w0lo, low_c, low_d, t0, nhi, nlo, xhi, xlo, y = refs[4:]
+    top_z, top_y = refs[:2]
+    lows = refs[2:6]
+    w0hi, w0lo, low_c, low_d, t0, nhi, nlo, xhi, xlo, y = refs[6:]
     row, _ = position()
     for n in range(2):
         for top, side in ((top_z, row % 2), (top_y, 1 - row % 2)):
             at = (2 * n + side + 3) % 4
             for m in range(2):
                 store_split(xhi, xlo, (block_at(4 * m + at), slice(None)), top[n, m * BLK : (m + 1) * BLK, :])
-        for low, z in ((low_y, row // 2), (low_z, 1 - row // 2)):
-            at = (2 * z + n + 3) % 4
-            for m in range(2):
-                y[block_at(4 * m + at), :] = low[n, m * BLK : (m + 1) * BLK, :]
+    for k in range(4):
+        at = ((row ^ k) + 3) % 4
+        for m in range(2):
+            y[block_at(4 * m + at), :] = lows[k][m * BLK : (m + 1) * BLK, :]
 
     def put(n, v):
         t0[256 * n : 256 * (n + 1), :] = v.astype(BF16)
@@ -469,7 +470,6 @@
 
     x_groups = [[4 * y + x for x in range(4)] for y in range(8)]
     row_groups = [[8 * r + c for c in range(8)] for r in range(4)]
-    y_groups = [[i, i + 8] for i in range(32) if not i & 8]
     z_groups = [[i, i + 16] for i in range(16)]
     low_half = col < 4
 
@@ -507,15 +507,14 @@
         (jax.ShapeDtypeStruct((256, 256), F32),),
         [quarter, small, block, rows_t],
     )
-    w11, q12, away, side_top = lax.optimization_barrier((w11, q12, away, side_top))
+    w11, q12, away, side_top, side_low = lax.optimization_barrier((w11, q12, away, side_top, side_low))
     q1, q2 = x_swap(q12[:, : 2 * BLK]), q12[:, 2 * BLK :]
-    far = swap(away, 4)
+    far, low_y = swap(away, 4), swap(side_low, 8)
     side_top = lax.all_gather(side_top, "tile", axis=0, axis_index_groups=z_groups)
     wa, top0 = call(
         kernel_a2, "panel_a2", 20_000_000_000, q0 + [w11], (mid, top_shape), [quarter, small, small, block, rows_t]
     )
-    wa, q2, q3, far, side_low, *q1 = lax.optimization_barrier((wa, q2, q3, far, side_low, *q1))
-    low_y = lax.all_gather(side_low, "tile", axis=0, axis_index_groups=y_groups)
+    wa, q2, q3, far, low_y, *q1 = lax.optimization_barrier((wa, q2, q3, far, low_y, *q1))
     q2 = x_swap(q2)
     q3_y, q3_z = swap(q3, 8), swap(q3, 16)
     w0hi, w0lo, top1 = call(
@@ -542,9 +541,9 @@
         (wide, mid, top_shape),
         [quarter, strip, strip, pltpu.VMEM((BLK, 512), F32), block, rows_t],
     )
-    wc, top_y, low_y, *rest = lax.optimization_barrier((wc, top_y, low_y, *pieces, *q3))
+    wc, top_y, *rest = lax.optimization_barrier((wc, top_y, *pieces, *q3))
     pieces, q3 = rest[:4], rest[4:]
-    low_z = swap(low_y, 16)
+    low_z = [swap(x, 16) for x in (side_low, low_y)]
     sub = jax.ShapeDtypeStruct((2, 96, 1024), BF16)
     (first,) = call(
         functools.partial(rows_kernel, 0),
@@ -563,7 +562,7 @@
         (wide, big, big, top_shape),
         [quarter, quarter, quarter, piece, piece, strip, strip, line, block, rows_t],
     )
-    w1hi, low_z = lax.optimization_barrier((w1hi, low_z))
+    w1hi, *low_z = lax.optimization_barrier((w1hi, *low_z))
     (second,) = call(
         functools.partial(rows_kernel, 1),
         "second_rows",
@@ -579,7 +578,7 @@
         columns_first,
         "columns_first",
         9_000_000_000,
-        [side_top, top_y, low_y, low_z, w0hi, w0lo, low_c, low_d],
+        [side_top, top_y, side_low, low_y, *low_z, w0hi, w0lo, low_c, low_d],
         (tall, tall, tall),
         [pltpu.VMEM((1024, 768), BF16)] * 2 + [pltpu.VMEM((1024, 768), F32)],
     )

time: 360 us -> 339 us (0.942); the launches traced: 362 us -> 332 us
  waiting for transfers between devices: 113 us -> 87.7 us
  starting transfers between devices: 63.2 us -> 57.4 us
    ppermute x2, waiting for transfers between devices: 51.8 us -> 37 us  [branch(): lax.ppermute(v, 'front', pairs)]
    ppermute x33 -> x35, waiting for transfers between devices: 57.4 us -> 46.6 us  [swap(): return lax.ppermute(x, 'tile', [(i, i ^ k) for i in range(32)])]
    ppermute x2, starting transfers between devices: 11.2 us -> 2.72 us  [branch(): lax.ppermute(v, 'front', pairs)]
    ppermute x33 -> x35, starting transfers between devices: 51.2 us -> 53.3 us  [swap(): return lax.ppermute(x, 'tile', [(i, i ^ k) for i in range(32)])]
  transfers between devices with their start and end apart: 43 -> 44, of which waited for: 17 -> 17; matrix products, arithmetic and copies ran while one was open for 3% -> 3% of each run, Pallas kernels for 38% -> 41%
where the time goes in v1:
time: 339 us; the launch traced here: 332 us
  Pallas kernels  155 us (46%)
  waiting for transfers between devices  87.7 us (26%)
  starting transfers between devices  57.4 us (17%)
  between operations  15.2 us (4%)
  local copies, waits for them, and re-layouts  12.5 us (4%)
  other arithmetic  4.74 us (1%)
    pallas_call x9, Pallas kernels, call(): pl.pallas_call(kernel, out_shape=outs, in_specs=[VMEM] * len(ins), out_sp...  131 us
    ppermute x35, starting transfers between devices, swap(): return lax.ppermute(x, 'tile', [(i, i ^ k) for i in range(32)])  53.3 us
    ppermute x35, waiting for transfers between devices, swap(): return lax.ppermute(x, 'tile', [(i, i ^ k) for i in range(32)])  46.6 us
    ppermute x2, waiting for transfers between devices, branch(): lax.ppermute(v, 'front', pairs)  37 us
    pallas_call x2, Pallas kernels, update(): pl.pallas_call(update_kernel, grid=(3,), out_shape=(jax.ShapeDtypeStruct(...  13.9 us
    pallas_call x1, Pallas kernels, per_device(): pl.pallas_call(merge_kernel, grid_spec=pltpu.PrefetchScalarGridSpec(num_s...  9.82 us
  transfers between devices with their start and end apart: 44, of which 17 were waited for; matrix products, arithmetic and copies ran while one was open for 3% of the time, Pallas kernels for 41%

profile of v1, /device:TPU:16, one launch (start us, length us, event | category | flops | bytes accessed | tf_op | source)
XLA Modules:
  0.0 332.5 jit_solution(10378181508552982196)
XLA Ops:
  9.3 3.0 collective-permute-done.30
  15.5 2.7 collective-permute-start.33
  25.5 2.6 fusion.5
  29.6 2.7 collective-permute-start.35
  38.9 2.7 collective-permute-done.35.refs_2_
  41.6 2.6 collective-permute-done.36.refs_3_
  44.2 9.5 %panel_a1.1.refs_4_ = f32[256,256]{1,0:T(8,128)} custom-call(f32[512,128]{1,0:T(8,128)} %copy-done.18, f32[512,128]{1,0:T(8,128)} %copy-done.30, f32[512,128]{1,0:T(8,128)} %collective-permute-done.35.refs_2_, f32[512,128]{1,0:T(8,128)} %collective-permute-done.36.refs_3_), custom_call_target="tpu_custom_call" | custom-call | flops 20000000000 | bytes 8000000 | tf_op jit(solution)/shard_map/panel_a1/pallas_call | solution.py:450
  55.8 2.8 collective-permute-start.45
  61.7 11.1 %panel_a2.1 = (f32[512,512]{1,0:T(8,128)}, bf16[128,256]{1,0:T(8,128)(2,1)}) custom-call(f32[512,128]{1,0:T(8,128)} %copy-done.18, f32[512,128]{1,0:T(8,128)} %copy-done.30, f32[512,128]{1,0:T(8,128)} %collective-permute-done.35.refs_2_, f32[512,128]{1,0:T(8,128)} %collective-permute-done.36.refs_3_, f32[256,256]{1,0:T(8,128)} %panel_a1.1.refs_4_), custom_call_target="tpu_custom_call" | custom-call | flops 20000000000 | bytes 8000000 | tf_op jit(solution)/shard_map/panel_a2/pallas_call | solution.py:450
  72.8 10.0 %collective-permute-done.44.refs_2_ = f32[512,256]{1,0:T(8,128)} collective-permute-done((f32[512,256]{1,0:T(8,128)S(1)}, f32[512,256]{1,0:T(8,128)}, u32[]{:S(2)}, u32[]{:S(2)}) %collective-permute-start.44) | collective-permute-done | bytes 524320 | tf_op jit(solution)/shard_map/ppermute | solution.py:447
  82.8 10.0 %collective-permute-done.42.refs_3_ = f32[256,768]{1,0:T(8,128)} collective-permute-done((f32[256,768]{1,0:T(8,128)}, f32[256,768]{1,0:T(8,128)}, u32[]{:S(2)}, u32[]{:S(2)}) %collective-permute-start.42) | collective-permute-done | bytes 786464 | tf_op jit(solution)/shard_map/ppermute | solution.py:447
  94.8 2.8 collective-permute-start.49
  99.9 24.2 %panel_b.1 = (bf16[1024,1024]{1,0:T(8,128)(2,1)}, bf16[1024,1024]{1,0:T(8,128)(2,1)}, bf16[128,256]{1,0:T(8,128)(2,1)}) custom-call(f32[512,256]{1,0:T(8,128)} %copy-done.10, f32[512,256]{1,0:T(8,128)} %collective-permute-done.43.refs_1_, f32[512,256]{1,0:T(8,128)} %collective-permute-done.44.refs_2_, f32[512,256]{1,0:T(8,128)} %collective-permute-done.45.refs_3_, ...), custom_call_target="tpu_custom_call" | custom-call | flops 32000000000 | bytes 8000000 | tf_op jit(solution)/shard_map/panel_b/pallas_call | solution.py:450
  125.5 2.6 collective-permute-done.49.refs_3_
  131.4 4.2 %collective-permute-start.52 = (f32[192,512]{1,0:T(8,128)S(1)}, f32[192,512]{1,0:T(8,128)S(1)}, u32[]{:S(2)}, u32[]{:S(2)}) collective-permute-start(f32[192,512]{1,0:T(8,128)S(1)} %bitcast.38), channel_id=1, source_target_pairs={{0,2},{1,3},{2,0},{3,1},{4,6},{5,7},{6,4},{7,5},{8,10},{9,11},{10,... | collective-permute-start | bytes 1179656 | tf_op jit(solution)/shard_map/ppermute | solution.py:447
  138.8 24.5 %panel_c.1 = (bf16[512,1024]{1,0:T(8,128)(2,1)}, f32[512,512]{1,0:T(8,128)}, bf16[128,256]{1,0:T(8,128)(2,1)}) custom-call(f32[512,384]{1,0:T(8,128)} %copy-done.9, f32[512,384]{1,0:T(8,128)} %collective-permute-done.47.refs_1_, f32[512,384]{1,0:T(8,128)} %collective-permute-done.48.refs_2_, f32[512,384]{1,0:T(8,128)} %collective-permute-done.49.refs_3_, ...), custom_call_target="tpu_custom_call" | custom-call | flops 35000000512 | bytes 8000000 | tf_op jit(solution)/shard_map/panel_c/pallas_call | solution.py:450
  167.3 5.0 %first_rows.1.refs_8_ = bf16[2,96,1024]{2,1,0:T(8,128)(2,1)} custom-call(f32[192,512]{1,0:T(8,128)} %bitcast.34, f32[192,512]{1,0:T(8,128)} %copy-done.2, f32[192,512]{1,0:T(8,128)} %copy-done.3, f32[192,512]{1,0:T(8,128)} %copy-done.4, bf16[1024,1024]{1,0:T(8,128)(2,1)} %get-tuple-element.156.refs_4_.refs_6_, ...), custom_call_target="tpu_custom_call" | custom-call | flops 1200000000 | bytes 8000000 | tf_op jit(solution)/shard_map/first_rows/pallas_call | solution.py:450
  172.3 31.0 %panel_d.1 = (bf16[512,1024]{1,0:T(8,128)(2,1)}, bf16[1024,1024]{1,0:T(8,128)(2,1)}, bf16[1024,1024]{1,0:T(8,128)(2,1)}, bf16[128,256]{1,0:T(8,128)(2,1)}) custom-call(f32[4,128,512]{2,1,0:T(8,128)} %bitcast.45, f32[4,128,512]{2,1,0:T(8,128)} %copy-done.27, f32[4,128,512]{2,1,0:T(8,128)} %collective-permute-done.54.refs_2_, f32[4,128,512]{2,1,0:T(8,128)} %copy-done.29, ...), custom_call_target="tpu_custom_call" | custom-call | flops 38000001024 | bytes 8000000 | tf_op jit(solution)/shard_map/panel_d/pallas_call | solution.py:450
  203.3 6.2 %second_rows.1 = bf16[2,96,1024]{2,1,0:T(8,128)(2,1)} custom-call(f32[192,512]{1,0:T(8,128)} %bitcast.35, f32[192,512]{1,0:T(8,128)} %copy-done.2, f32[192,512]{1,0:T(8,128)} %copy-done.3, f32[192,512]{1,0:T(8,128)} %copy-done.4, bf16[1024,1024]{1,0:T(8,128)(2,1)} %get-tuple-element.176.refs_4_.whi, bf16[1024,1024]{1,0:T(8,128)(2,1)} %get-tuple-element.177.refs_5_.wlo, ...), custom_call_target="tpu_custom_call" | custom-call | flops 1700000000 | bytes 8000000 | tf_op jit(solution)/shard_map/second_rows/pallas_call | solution.py:450
  211.4 12.0 %columns_first.1 = (bf16[1024,768]{1,0:T(8,128)(2,1)}, bf16[1024,768]{1,0:T(8,128)(2,1)}, bf16[1024,768]{1,0:T(8,128)(2,1)}) custom-call(f32[2,256,768]{2,1,0:T(8,128)} %bitcast.41, f32[2,256,768]{2,1,0:T(8,128)} %copy-done.26, f32[256,768]{1,0:T(8,128)} %get-tuple-element.140.refs_2_, f32[256,768]{1,0:T(8,128)} %collective-permute-done.42.refs_3_, ...), custom_call_target="tpu_custom_call" | custom-call | flops 8999999488 | bytes 8000000 | tf_op jit(solution)/shard_map/columns_first/pallas_call | solution.py:450
  224.7 3.5 %collective-permute-start.60 = (bf16[2,96,1024]{2,1,0:T(8,128)(2,1)S(1)}, bf16[2,96,1024]{2,1,0:T(8,128)(2,1)S(1)}, u32[]{:S(2)}, u32[]{:S(2)}) collective-permute-start(bf16[2,96,1024]{2,1,0:T(8,128)(2,1)S(1)} %pad_maximum_fusion.1.refs_0_), channel_id=1, source_target_pairs={{0,2},{1,3},{2,0},{3,1},{4,6},{5,7},{6,4},{7,5},{8,10},{9,11},{10,... | collective-permute-start | bytes 1179656 | tf_op jit(solution)/shard_map/ppermute | solution.py:447
  229.4 7.5 %columns_second.1.refs_5_ = bf16[1024,768]{1,0:T(8,128)(2,1)} custom-call(bf16[1024,768]{1,0:T(8,128)(2,1)} %get-tuple-element.187.nhi, bf16[1024,768]{1,0:T(8,128)(2,1)} %get-tuple-element.188.nlo, bf16[1024,1024]{1,0:T(8,128)(2,1)} %get-tuple-element.176.refs_4_.whi, bf16[1024,1024]{1,0:T(8,128)(2,1)} %get-tuple-element.177.refs_5_.wlo), custom_call_target="tpu_custom_call" | custom-call | flops 8999999488 | bytes 8000000 | tf_op jit(solution)/shard_map/columns_second/pallas_call | solution.py:450
  237.0 8.7 %collective-permute-done.60.refs_2_ = bf16[2,96,1024]{2,1,0:T(8,128)(2,1)S(1)} collective-permute-done((bf16[2,96,1024]{2,1,0:T(8,128)(2,1)S(1)}, bf16[2,96,1024]{2,1,0:T(8,128)(2,1)S(1)}, u32[]{:S(2)}, u32[]{:S(2)}) %collective-permute-start.60) | collective-permute-done | bytes 393248 | tf_op jit(solution)/shard_map/ppermute | solution.py:447
  245.7 2.6 collective-permute-done.61.refs_3_
  249.0 6.9 %update.2 = (bf16[768,768]{1,0:T(8,128)(2,1)S(1)}, bf16[768,256]{1,0:T(8,128)(2,1)}) custom-call(bf16[8,2,96,1024]{3,2,1,0:T(8,128)(2,1)} %bitcast.29, bf16[2,96,1024]{2,1,0:T(8,128)(2,1)} %copy-done.1, bf16[2,96,1024]{2,1,0:T(8,128)(2,1)} %copy-done.13, bf16[2,96,1024]{2,1,0:T(8,128)(2,1)} %copy-done.14, bf16[2,96,1024]{2,1,0:T(8,128)(2,1)} %copy-done.15, ...), custom_call_target="tpu_custom_call" | custom-call | flops 2500000000 | bytes 9000000 | tf_op jit(solution)/shard_map/update/pallas_call | solution.py:597
  255.9 2.7 collective-permute-start.63
  262.0 19.9 %conditional.2 = (bf16[768,768]{1,0:T(8,128)(2,1)}) conditional(s32[]{:T(128)} %clamp.4, () %tuple.122, bf16[768,768]{1,0:T(8,128)(2,1)S(1)} %get-tuple-element.191.refs_0_, bf16[768,768]{1,0:T(8,128)(2,1)S(1)} %get-tuple-element.191.refs_0_, bf16[768,768]{1,0:T(8,128)(2,1)S(1)} %get-tuple-element.191.refs_0_, ...), branch_computations={%region_1.2_spmd, %region_2.3_spmd, %region_3.4_spmd, %region_4.5_... | conditional | bytes 4718640 | solution.py:469
  263.3 18.4 %collective-permute-done.5 = bf16[768,768]{1,0:T(8,128)(2,1)} collective-permute-done((bf16[768,768]{1,0:T(8,128)(2,1)S(1)}, bf16[768,768]{1,0:T(8,128)(2,1)}, u32[]{:S(2)}, u32[]{:S(2)}) %collective-permute-start.5) | collective-permute-done | bytes 1179680 | tf_op jit(solution)/shard_map/cond/branch_6_fun/ppermute | solution.py:467
  282.8 7.0 %update.3 = (bf16[768,768]{1,0:T(8,128)(2,1)}, bf16[768,256]{1,0:T(8,128)(2,1)}) custom-call(bf16[8,2,96,1024]{3,2,1,0:T(8,128)(2,1)} %bitcast.30, bf16[2,96,1024]{2,1,0:T(8,128)(2,1)} %copy-done, bf16[2,96,1024]{2,1,0:T(8,128)(2,1)} %copy-done.11, bf16[2,96,1024]{2,1,0:T(8,128)(2,1)} %copy-done.12, bf16[2,96,1024]{2,1,0:T(8,128)(2,1)} %collective-permute-done.64.refs_3_, ...), custom_call_target="tpu_custom_call" | custom-call | flops 2500000000 | bytes 9000000 | tf_op jit(solution)/shard_map/update/pallas_call | solution.py:597
  290.0 20.1 %conditional.3 = (bf16[768,768]{1,0:T(8,128)(2,1)}) conditional(s32[]{:T(128)} %clamp.4, () %tuple.125, bf16[768,768]{1,0:T(8,128)(2,1)} %get-tuple-element.198.refs_1_, bf16[768,768]{1,0:T(8,128)(2,1)} %get-tuple-element.198.refs_1_, bf16[768,768]{1,0:T(8,128)(2,1)} %get-tuple-element.198.refs_1_, ...), branch_computations={%region_17.18_spmd, %region_18.19_spmd, %region_19.20_spmd, %regio... | conditional | bytes 4718640 | solution.py:469
  291.5 18.6 %collective-permute-done.20 = bf16[768,768]{1,0:T(8,128)(2,1)} collective-permute-done((bf16[768,768]{1,0:T(8,128)(2,1)}, bf16[768,768]{1,0:T(8,128)(2,1)}, u32[]{:S(2)}, u32[]{:S(2)}) %collective-permute-start.20) | collective-permute-done | bytes 1179680 | tf_op jit(solution)/shard_map/cond/branch_6_fun/ppermute | solution.py:467
  315.9 9.8 %merge.1 = f32[2048,1024]{1,0:T(8,128)} custom-call(s32[4]{0:T(128)} %owner.1, s32[4,48]{1,0:T(4,128)} %block_map.1, bf16[2048,1024]{1,0:T(8,128)(2,1)} %bitcast.33, bf16[768,768]{1,0:T(8,128)(2,1)S(1)} %get-tuple-element.191.refs_0_, bf16[768,768]{1,0:T(8,128)(2,1)} %get-tuple-element.198.refs_1_, bf16[768,768]{1,0:T(8,128)(2,1)} %copy-done.6, ...), custom_call_target="tpu_custom_call" | custom-call | flops 10000000 | bytes 22000000 | tf_op jit(solution)/shard_map/merge/pallas_call | solution.py:638
  (163 shorter events, 59.3 us)
Async XLA Ops:
  7.2 85.7 %all-gather.7.cloned.1.call-start = ((), (), s32[]{:S(2)}) async-start(), calls=%async_computation | async-start | bytes 1310720 | tf_op jit(solution)/shard_map/all_gather | solution.py:494
  33.0 20.7 %collective-permute-start.38 = (f32[128,640]{1,0:T(8,128)S(1)}, f32[128,640]{1,0:T(8,128)S(1)}, u32[]{:S(2)}, u32[]{:S(2)}) collective-permute-start(f32[128,640]{1,0:T(8,128)S(1)} %get-tuple-element.216), channel_id=1, source_target_pairs={{0,8},{1,9},{2,10},{3,11},{4,12},{5,13},{6,14},{7,15},{8,0},{9,1},... | collective-permute-start | bytes 983048 | tf_op jit(solution)/shard_map/ppermute | solution.py:447
  35.1 18.5 %collective-permute-start.39 = (f32[128,640]{1,0:T(8,128)S(1)}, f32[128,640]{1,0:T(8,128)S(1)}, u32[]{:S(2)}, u32[]{:S(2)}) collective-permute-start(f32[128,640]{1,0:T(8,128)S(1)} %get-tuple-element.216), channel_id=1, source_target_pairs={{0,16},{1,17},{2,18},{3,19},{4,20},{5,21},{6,22},{7,23},{8,24},{9,... | collective-permute-start | bytes 983048 | tf_op jit(solution)/shard_map/ppermute | solution.py:447
  35.9 88.2 %all-gather.9.cloned.1.call-start = ((), (), s32[]{:S(2)}) async-start(), calls=%async_computation.1 | async-start | bytes 2359296 | tf_op jit(solution)/shard_map/all_gather | solution.py:513
  36.4 17.2 %collective-permute-start.40 = (f32[128,640]{1,0:T(8,128)S(1)}, f32[128,640]{1,0:T(8,128)S(1)}, u32[]{:S(2)}, u32[]{:S(2)}) collective-permute-start(f32[128,640]{1,0:T(8,128)S(1)} %get-tuple-element.216), channel_id=1, source_target_pairs={{0,24},{1,25},{2,26},{3,27},{4,28},{5,29},{6,30},{7,31},{8,16},{9,... | collective-permute-start | bytes 983048 | tf_op jit(solution)/shard_map/ppermute | solution.py:447
  53.8 19.0 %collective-permute-start.43 = (f32[512,256]{1,0:T(8,128)S(1)}, f32[512,256]{1,0:T(8,128)}, u32[]{:S(2)}, u32[]{:S(2)}) collective-permute-start(f32[512,256]{1,0:T(8,128)S(1)} %slice.75.refs_0_), channel_id=1, source_target_pairs={{0,1},{1,0},{2,3},{3,2},{4,5},{5,4},{6,7},{7,6},{8,9},{9,8},{10,11... | collective-permute-start | bytes 1572872 | tf_op jit(solution)/shard_map/ppermute | solution.py:447
  53.9 28.9 %collective-permute-start.44 = (f32[512,256]{1,0:T(8,128)S(1)}, f32[512,256]{1,0:T(8,128)}, u32[]{:S(2)}, u32[]{:S(2)}) collective-permute-start(f32[512,256]{1,0:T(8,128)S(1)} %slice.75.refs_0_), channel_id=1, source_target_pairs={{0,2},{1,3},{2,0},{3,1},{4,6},{5,7},{6,4},{7,5},{8,10},{9,11},{10,... | collective-permute-start | bytes 1572872 | tf_op jit(solution)/shard_map/ppermute | solution.py:447
  55.8 27.0 %collective-permute-start.45 = (f32[512,256]{1,0:T(8,128)S(1)}, f32[512,256]{1,0:T(8,128)}, u32[]{:S(2)}, u32[]{:S(2)}) collective-permute-start(f32[512,256]{1,0:T(8,128)S(1)} %slice.75.refs_0_), channel_id=1, source_target_pairs={{0,3},{1,2},{2,1},{3,0},{4,7},{5,6},{6,5},{7,4},{8,11},{9,10},{10,... | collective-permute-start | bytes 1572872 | tf_op jit(solution)/shard_map/ppermute | solution.py:447
  58.6 24.3 %collective-permute-start.41 = (f32[2,384,256]{2,1,0:T(8,128)}, f32[2,384,256]{2,1,0:T(8,128)}, u32[]{:S(2)}, u32[]{:S(2)}) collective-permute-start(f32[2,384,256]{2,1,0:T(8,128)} %get-tuple-element.139), channel_id=1, source_target_pairs={{0,4},{1,5},{2,6},{3,7},{4,0},{5,1},{6,2},{7,3},{8,12},{9,13},{10,... | collective-permute-start | bytes 2359304 | tf_op jit(solution)/shard_map/ppermute | solution.py:447
  58.9 34.0 %collective-permute-start.42 = (f32[256,768]{1,0:T(8,128)}, f32[256,768]{1,0:T(8,128)}, u32[]{:S(2)}, u32[]{:S(2)}) collective-permute-start(f32[256,768]{1,0:T(8,128)} %get-tuple-element.140.refs_2_), channel_id=1, source_target_pairs={{0,8},{1,9},{2,10},{3,11},{4,12},{5,13},{6,14},{7,15},{8,0},{9,1},... | collective-permute-start | bytes 2359304 | tf_op jit(solution)/shard_map/ppermute | solution.py:447
  61.1 187.2 %all-gather.11.cloned.1.call-start = ((), (), s32[]{:S(2)}) async-start(), calls=%async_computation.2 | async-start | bytes 3538944 | tf_op jit(solution)/shard_map/all_gather | solution.py:556
  92.8 31.2 %collective-permute-start.47 = (f32[512,384]{1,0:T(8,128)S(1)}, f32[512,384]{1,0:T(8,128)}, u32[]{:S(2)}, u32[]{:S(2)}) collective-permute-start(f32[512,384]{1,0:T(8,128)S(1)} %slice.70.refs_0_), channel_id=1, source_target_pairs={{0,1},{1,0},{2,3},{3,2},{4,5},{5,4},{6,7},{7,6},{8,9},{9,8},{10,11... | collective-permute-start | bytes 2359304 | tf_op jit(solution)/shard_map/ppermute | solution.py:447
  92.8 32.7 %collective-permute-start.48 = (f32[512,384]{1,0:T(8,128)S(1)}, f32[512,384]{1,0:T(8,128)}, u32[]{:S(2)}, u32[]{:S(2)}) collective-permute-start(f32[512,384]{1,0:T(8,128)S(1)} %slice.70.refs_0_), channel_id=1, source_target_pairs={{0,2},{1,3},{2,0},{3,1},{4,6},{5,7},{6,4},{7,5},{8,10},{9,11},{10,... | collective-permute-start | bytes 2359304 | tf_op jit(solution)/shard_map/ppermute | solution.py:447
  94.8 33.3 %collective-permute-start.49 = (f32[512,384]{1,0:T(8,128)S(1)}, f32[512,384]{1,0:T(8,128)}, u32[]{:S(2)}, u32[]{:S(2)}) collective-permute-start(f32[512,384]{1,0:T(8,128)S(1)} %slice.70.refs_0_), channel_id=1, source_target_pairs={{0,3},{1,2},{2,1},{3,0},{4,7},{5,6},{6,5},{7,4},{8,11},{9,10},{10,... | collective-permute-start | bytes 2359304 | tf_op jit(solution)/shard_map/ppermute | solution.py:447
  97.5 30.6 %collective-permute-start.46 = (f32[4,128,512]{2,1,0:T(8,128)}, f32[4,128,512]{2,1,0:T(8,128)S(1)}, u32[]{:S(2)}, u32[]{:S(2)}) collective-permute-start(f32[4,128,512]{2,1,0:T(8,128)} %bitcast.43), channel_id=1, source_target_pairs={{0,8},{1,9},{2,10},{3,11},{4,12},{5,13},{6,14},{7,15},{8,0},{9,1},... | collective-permute-start | bytes 3145736 | tf_op jit(solution)/shard_map/ppermute | solution.py:447
  99.2 38.9 %collective-permute-start.54 = (f32[4,128,512]{2,1,0:T(8,128)}, f32[4,128,512]{2,1,0:T(8,128)}, u32[]{:S(2)}, u32[]{:S(2)}) collective-permute-start(f32[4,128,512]{2,1,0:T(8,128)} %bitcast.44), channel_id=1, source_target_pairs={{0,16},{1,17},{2,18},{3,19},{4,20},{5,21},{6,22},{7,23},{8,24},{9,... | collective-permute-start | bytes 3145736 | tf_op jit(solution)/shard_map/ppermute | solution.py:447
  131.4 31.9 %collective-permute-start.51 = (f32[192,512]{1,0:T(8,128)S(1)}, f32[192,512]{1,0:T(8,128)S(1)}, u32[]{:S(2)}, u32[]{:S(2)}) collective-permute-start(f32[192,512]{1,0:T(8,128)S(1)} %bitcast.39), channel_id=1, source_target_pairs={{0,1},{1,0},{2,3},{3,2},{4,5},{5,4},{6,7},{7,6},{8,9},{9,8},{10,11... | collective-permute-start | bytes 1179656 | tf_op jit(solution)/shard_map/ppermute | solution.py:447
  131.4 33.5 %collective-permute-start.52 = (f32[192,512]{1,0:T(8,128)S(1)}, f32[192,512]{1,0:T(8,128)S(1)}, u32[]{:S(2)}, u32[]{:S(2)}) collective-permute-start(f32[192,512]{1,0:T(8,128)S(1)} %bitcast.38), channel_id=1, source_target_pairs={{0,2},{1,3},{2,0},{3,1},{4,6},{5,7},{6,4},{7,5},{8,10},{9,11},{10,... | collective-permute-start | bytes 1179656 | tf_op jit(solution)/shard_map/ppermute | solution.py:447
  135.6 30.0 %collective-permute-start.53 = (f32[192,512]{1,0:T(8,128)S(1)}, f32[192,512]{1,0:T(8,128)S(1)}, u32[]{:S(2)}, u32[]{:S(2)}) collective-permute-start(f32[192,512]{1,0:T(8,128)S(1)} %bitcast.37), channel_id=1, source_target_pairs={{0,3},{1,2},{2,1},{3,0},{4,7},{5,6},{6,5},{7,4},{8,11},{9,10},{10,... | collective-permute-start | bytes 1179656 | tf_op jit(solution)/shard_map/ppermute | solution.py:447
  136.1 29.7 %collective-permute-start.50 = (f32[2,256,768]{2,1,0:T(8,128)S(1)}, f32[2,256,768]{2,1,0:T(8,128)S(1)}, u32[]{:S(2)}, u32[]{:S(2)}) collective-permute-start(f32[2,256,768]{2,1,0:T(8,128)S(1)} %bitcast.42), channel_id=1, source_target_pairs={{0,8},{1,9},{2,10},{3,11},{4,12},{5,13},{6,14},{7,15},{8,0},{9,1},... | collective-permute-start | bytes 4718600 | tf_op jit(solution)/shard_map/ppermute | solution.py:447
  138.1 27.6 %collective-permute-start.55 = (f32[4,128,512]{2,1,0:T(8,128)S(1)}, f32[4,128,512]{2,1,0:T(8,128)S(1)}, u32[]{:S(2)}, u32[]{:S(2)}) collective-permute-start(f32[4,128,512]{2,1,0:T(8,128)S(1)} %copy-done.28), channel_id=1, source_target_pairs={{0,16},{1,17},{2,18},{3,19},{4,20},{5,21},{6,22},{7,23},{8,24},{9,... | collective-permute-start | bytes 3145736 | tf_op jit(solution)/shard_map/ppermute | solution.py:447
  163.3 40.0 %collective-permute-start.56 = (f32[256,768]{1,0:T(8,128)}, f32[256,768]{1,0:T(8,128)}, u32[]{:S(2)}, u32[]{:S(2)}) collective-permute-start(f32[256,768]{1,0:T(8,128)} %get-tuple-element.140.refs_2_), channel_id=1, source_target_pairs={{0,16},{1,17},{2,18},{3,19},{4,20},{5,21},{6,22},{7,23},{8,24},{9,... | collective-permute-start | bytes 2359304 | tf_op jit(solution)/shard_map/ppermute | solution.py:447
  164.9 38.4 %collective-permute-start.57 = (f32[256,768]{1,0:T(8,128)}, f32[256,768]{1,0:T(8,128)}, u32[]{:S(2)}, u32[]{:S(2)}) collective-permute-start(f32[256,768]{1,0:T(8,128)} %collective-permute-done.42.refs_3_), channel_id=1, source_target_pairs={{0,16},{1,17},{2,18},{3,19},{4,20},{5,21},{6,22},{7,23},{8,24},{9,... | collective-permute-start | bytes 2359304 | tf_op jit(solution)/shard_map/ppermute | solution.py:447
  224.7 21.0 %collective-permute-start.60 = (bf16[2,96,1024]{2,1,0:T(8,128)(2,1)S(1)}, bf16[2,96,1024]{2,1,0:T(8,128)(2,1)S(1)}, u32[]{:S(2)}, u32[]{:S(2)}) collective-permute-start(bf16[2,96,1024]{2,1,0:T(8,128)(2,1)S(1)} %pad_maximum_fusion.1.refs_0_), channel_id=1, source_target_pairs={{0,2},{1,3},{2,0},{3,1},{4,6},{5,7},{6,4},{7,5},{8,10},{9,11},{10,... | collective-permute-start | bytes 1179656 | tf_op jit(solution)/shard_map/ppermute | solution.py:447
  228.1 20.1 %collective-permute-start.61 = (bf16[2,96,1024]{2,1,0:T(8,128)(2,1)S(1)}, bf16[2,96,1024]{2,1,0:T(8,128)(2,1)S(1)}, u32[]{:S(2)}, u32[]{:S(2)}) collective-permute-start(bf16[2,96,1024]{2,1,0:T(8,128)(2,1)S(1)} %pad_maximum_fusion.1.refs_0_), channel_id=1, source_target_pairs={{0,3},{1,2},{2,1},{3,0},{4,7},{5,6},{6,5},{7,4},{8,11},{9,10},{10,... | collective-permute-start | bytes 1179656 | tf_op jit(solution)/shard_map/ppermute | solution.py:447
  255.9 26.0 %collective-permute-start.62 = (bf16[2,96,1024]{2,1,0:T(8,128)(2,1)S(1)}, bf16[2,96,1024]{2,1,0:T(8,128)(2,1)S(1)}, u32[]{:S(2)}, u32[]{:S(2)}) collective-permute-start(bf16[2,96,1024]{2,1,0:T(8,128)(2,1)S(1)} %pad_maximum_fusion.2.refs_0_), channel_id=1, source_target_pairs={{0,1},{1,0},{2,3},{3,2},{4,5},{5,4},{6,7},{7,6},{8,9},{9,8},{10,11... | collective-permute-start | bytes 1179656 | tf_op jit(solution)/shard_map/ppermute | solution.py:447
  255.9 26.1 %collective-permute-start.63 = (bf16[2,96,1024]{2,1,0:T(8,128)(2,1)S(1)}, bf16[2,96,1024]{2,1,0:T(8,128)(2,1)S(1)}, u32[]{:S(2)}, u32[]{:S(2)}) collective-permute-start(bf16[2,96,1024]{2,1,0:T(8,128)(2,1)S(1)} %pad_maximum_fusion.2.refs_0_), channel_id=1, source_target_pairs={{0,2},{1,3},{2,0},{3,1},{4,6},{5,7},{6,4},{7,5},{8,10},{9,11},{10,... | collective-permute-start | bytes 1179656 | tf_op jit(solution)/shard_map/ppermute | solution.py:447
  258.6 23.4 %collective-permute-start.64 = (bf16[2,96,1024]{2,1,0:T(8,128)(2,1)S(1)}, bf16[2,96,1024]{2,1,0:T(8,128)(2,1)}, u32[]{:S(2)}, u32[]{:S(2)}) collective-permute-start(bf16[2,96,1024]{2,1,0:T(8,128)(2,1)S(1)} %pad_maximum_fusion.2.refs_0_), channel_id=1, source_target_pairs={{0,3},{1,2},{2,1},{3,0},{4,7},{5,6},{6,5},{7,4},{8,11},{9,10},{10,... | collective-permute-start | bytes 1179656 | tf_op jit(solution)/shard_map/ppermute | solution.py:447
  261.9 48.9 %collective-permute-start.65 = (bf16[768,768]{1,0:T(8,128)(2,1)S(1)}, bf16[768,768]{1,0:T(8,128)(2,1)S(1)}, u32[]{:S(2)}, u32[]{:S(2)}) collective-permute-start(bf16[768,768]{1,0:T(8,128)(2,1)S(1)} %get-tuple-element.191.refs_0_), channel_id=1, source_target_pairs={{0,32},{32,0},{64,96},{96,64},{1,33},{33,1},{65,97},{97,65},{2,34}... | collective-permute-start | bytes 3538952 | tf_op jit(solution)/shard_map/ppermute | solution.py:462
  262.0 19.7 %collective-permute-start.5 = (bf16[768,768]{1,0:T(8,128)(2,1)S(1)}, bf16[768,768]{1,0:T(8,128)(2,1)}, u32[]{:S(2)}, u32[]{:S(2)}) collective-permute-start(bf16[768,768]{1,0:T(8,128)(2,1)S(1)} %param.6), channel_id=1, source_target_pairs={{32,96},{64,0},{33,97},{65,1},{34,98},{66,2},{35,99},{67,3},{36,10... | collective-permute-start | bytes 3538952 | tf_op jit(solution)/shard_map/cond/branch_6_fun/ppermute | solution.py:467
  289.9 23.2 %collective-permute-start.66 = (bf16[768,768]{1,0:T(8,128)(2,1)}, bf16[768,768]{1,0:T(8,128)(2,1)}, u32[]{:S(2)}, u32[]{:S(2)}) collective-permute-start(bf16[768,768]{1,0:T(8,128)(2,1)} %get-tuple-element.198.refs_1_), channel_id=1, source_target_pairs={{0,32},{32,0},{64,96},{96,64},{1,33},{33,1},{65,97},{97,65},{2,34}... | collective-permute-start | bytes 3538952 | tf_op jit(solution)/shard_map/ppermute | solution.py:462
  290.0 20.0 %collective-permute-start.20 = (bf16[768,768]{1,0:T(8,128)(2,1)}, bf16[768,768]{1,0:T(8,128)(2,1)}, u32[]{:S(2)}, u32[]{:S(2)}) collective-permute-start(bf16[768,768]{1,0:T(8,128)(2,1)} %param.22), channel_id=1, source_target_pairs={{32,96},{64,0},{33,97},{65,1},{34,98},{66,2},{35,99},{67,3},{36,10... | collective-permute-start | bytes 3538952 | tf_op jit(solution)/shard_map/cond/branch_6_fun/ppermute | solution.py:467
  (43 other events, 442.7 us)
Sparse Core Ops, SparseCore 0:
  36.0 28.6 all-gather.6
  66.3 32.8 all-gather.8
  172.4 45.8 all-gather.10

commit v2 on v0

--- a/solution.py
+++ b/solution.py
@@ -337,12 +337,12 @@
 
 
 def columns_first(*refs):
-    top_z, top_y, low_y, low_z = refs[:4]
+    tops, top_y, low_y, low_z = refs[:4]
     w0hi, w0lo, low_c, low_d, t0, nhi, nlo, xhi, xlo, y = refs[4:]
     row, _ = position()
     for n in range(2):
-        for top, side in ((top_z, row % 2), (top_y, 1 - row % 2)):
-            at = (2 * n + side + 3) % 4
+        for top, flip in ((tops, 2 * n), (top_y, 2 * n + 1)):
+            at = ((row ^ flip) + 3) % 4
             for m in range(2):
                 store_split(xhi, xlo, (block_at(4 * m + at), slice(None)), top[n, m * BLK : (m + 1) * BLK, :])
         for low, z in ((low_y, row // 2), (low_z, 1 - row // 2)):
@@ -470,7 +470,6 @@
     x_groups = [[4 * y + x for x in range(4)] for y in range(8)]
     row_groups = [[8 * r + c for c in range(8)] for r in range(4)]
     y_groups = [[i, i + 8] for i in range(32) if not i & 8]
-    z_groups = [[i, i + 16] for i in range(16)]
     low_half = col < 4
 
     def column_swap(x):
@@ -507,15 +506,14 @@
         (jax.ShapeDtypeStruct((256, 256), F32),),
         [quarter, small, block, rows_t],
     )
-    w11, q12, away, side_top = lax.optimization_barrier((w11, q12, away, side_top))
+    w11, q12, away, side_top, side_low = lax.optimization_barrier((w11, q12, away, side_top, side_low))
     q1, q2 = x_swap(q12[:, : 2 * BLK]), q12[:, 2 * BLK :]
-    far = swap(away, 4)
-    side_top = lax.all_gather(side_top, "tile", axis=0, axis_index_groups=z_groups)
+    far, top_z = swap(away, 4), swap(side_top, 16)
+    low_y = lax.all_gather(side_low, "tile", axis=0, axis_index_groups=y_groups)
     wa, top0 = call(
         kernel_a2, "panel_a2", 20_000_000_000, q0 + [w11], (mid, top_shape), [quarter, small, small, block, rows_t]
     )
-    wa, q2, q3, far, side_low, *q1 = lax.optimization_barrier((wa, q2, q3, far, side_low, *q1))
-    low_y = lax.all_gather(side_low, "tile", axis=0, axis_index_groups=y_groups)
+    wa, q2, q3, far, top_z, *q1 = lax.optimization_barrier((wa, q2, q3, far, top_z, *q1))
     q2 = x_swap(q2)
     q3_y, q3_z = swap(q3, 8), swap(q3, 16)
     w0hi, w0lo, top1 = call(
@@ -526,14 +524,15 @@
         (big, big, top_shape),
         [quarter, quarter, quarter, piece, piece, line, block, rows_t],
     )
-    w0hi, far, q3_y, side_top, *q2 = lax.optimization_barrier((w0hi, far, q3_y, side_top, *q2))
+    w0hi, far, q3_y, *q2 = lax.optimization_barrier((w0hi, far, q3_y, *q2))
     q3 = [q3, q3_y, q3_z, swap(q3_y, 16)]
     both = jnp.concatenate([near, far], 2).reshape(2, 4, 96, 512)
     pieces = [
         lax.dynamic_index_in_dim(both, (col % 4) ^ k, 1, keepdims=False).reshape(192, 512) for k in range(4)
     ]
     pieces = pieces[:1] + [swap(pieces[k], k) for k in range(1, 4)]
-    top_y = swap(side_top, 8)
+    tops = jnp.stack([side_top, top_z])
+    top_y = swap(tops, 8)
     low_c, wc, top2 = call(
         kernel_c,
         "panel_c",
@@ -574,12 +573,12 @@
     )
     pair = swap(second, 4)
     tall = jax.ShapeDtypeStruct((1024, 768), BF16)
-    second, side_top = lax.optimization_barrier((second, side_top))
+    second, tops = lax.optimization_barrier((second, tops))
     t0, nhi, nlo = call(
         columns_first,
         "columns_first",
         9_000_000_000,
-        [side_top, top_y, low_y, low_z, w0hi, w0lo, low_c, low_d],
+        [tops, top_y, low_y, low_z, w0hi, w0lo, low_c, low_d],
         (tall, tall, tall),
         [pltpu.VMEM((1024, 768), BF16)] * 2 + [pltpu.VMEM((1024, 768), F32)],
     )

time: 360 us -> 339 us (0.942)
  waiting for transfers between devices: 113 us -> 94.8 us
  starting transfers between devices: 63.2 us -> 59.1 us
    ppermute x33 -> x34, waiting for transfers between devices: 57.4 us -> 34.4 us  [swap(): return lax.ppermute(x, 'tile', [(i, i ^ k) for i in range(32)])]
    ppermute x2, waiting for transfers between devices: 51.8 us -> 56.3 us  [branch(): lax.ppermute(v, 'front', pairs)]
    ppermute x2, starting transfers between devices: 11.2 us -> 7.51 us  [branch(): lax.ppermute(v, 'front', pairs)]
    ppermute x33 -> x34, starting transfers between devices: 51.2 us -> 50.7 us  [swap(): return lax.ppermute(x, 'tile', [(i, i ^ k) for i in range(32)])]
  transfers between devices with their start and end apart: 43 -> 43, of which waited for: 17 -> 15; matrix products, arithmetic and copies ran while one was open for 3% -> 4% of each run, Pallas kernels for 38% -> 40%
where the time goes in v2:
time: 339 us; the launch traced here: 343 us
  Pallas kernels  154 us (45%)
  waiting for transfers between devices  94.8 us (28%)
  starting transfers between devices  59.1 us (17%)
  between operations  15.3 us (5%)
  local copies, waits for them, and re-layouts  11.5 us (3%)
  other arithmetic  8.01 us (2%)
    pallas_call x9, Pallas kernels, call(): pl.pallas_call(kernel, out_shape=outs, in_specs=[VMEM] * len(ins), out_sp...  131 us
    ppermute x2, waiting for transfers between devices, branch(): lax.ppermute(v, 'front', pairs)  56.3 us
    ppermute x34, starting transfers between devices, swap(): return lax.ppermute(x, 'tile', [(i, i ^ k) for i in range(32)])  50.7 us
    ppermute x34, waiting for transfers between devices, swap(): return lax.ppermute(x, 'tile', [(i, i ^ k) for i in range(32)])  34.4 us
    pallas_call x2, Pallas kernels, update(): pl.pallas_call(update_kernel, grid=(3,), out_shape=(jax.ShapeDtypeStruct(...  13.9 us
    pallas_call x1, Pallas kernels, per_device(): pl.pallas_call(merge_kernel, grid_spec=pltpu.PrefetchScalarGridSpec(num_s...  8.89 us
    ppermute x2, starting transfers between devices, branch(): lax.ppermute(v, 'front', pairs)  7.51 us
  transfers between devices with their start and end apart: 43, of which 15 were waited for; matrix products, arithmetic and copies ran while one was open for 4% of the time, Pallas kernels for 40%

profile of v2, /device:TPU:16, one launch (start us, length us, event | category | flops | bytes accessed | tf_op | source)
XLA Modules:
  0.0 343.1 jit_solution(18130041633832463147)
XLA Ops:
  9.3 3.0 collective-permute-done.30
  15.5 2.7 collective-permute-start.33
  30.0 2.7 collective-permute-start.35
  39.3 2.8 collective-permute-done.35.refs_2_
  42.1 2.7 collective-permute-done.36.refs_3_
  44.7 9.5 %panel_a1.1.refs_4_ = f32[256,256]{1,0:T(8,128)} custom-call(f32[512,128]{1,0:T(8,128)} %pad_maximum_fusion.4.refs_0_, f32[512,128]{1,0:T(8,128)} %copy-done.29, f32[512,128]{1,0:T(8,128)} %copy-done.30, f32[512,128]{1,0:T(8,128)} %collective-permute-done.36.refs_3_), custom_call_target="tpu_custom_call" | custom-call | flops 20000000000 | bytes 8000000 | tf_op jit(solution)/shard_map/panel_a1/pallas_call | solution.py:449
  58.1 2.8 collective-permute-start.45
  61.9 11.1 %panel_a2.1 = (f32[512,512]{1,0:T(8,128)}, bf16[128,256]{1,0:T(8,128)(2,1)}) custom-call(f32[512,128]{1,0:T(8,128)} %pad_maximum_fusion.4.refs_0_, f32[512,128]{1,0:T(8,128)} %copy-done.29, f32[512,128]{1,0:T(8,128)} %copy-done.30, f32[512,128]{1,0:T(8,128)} %collective-permute-done.36.refs_3_, f32[256,256]{1,0:T(8,128)} %panel_a1.1.refs_4_), custom_call_target="tpu_custom_call" | custom-call | flops 20000000000 | bytes 8000000 | tf_op jit(solution)/shard_map/panel_a2/pallas_call | solution.py:449
  73.9 9.4 %collective-permute-done.44.refs_2_ = f32[512,256]{1,0:T(8,128)} collective-permute-done((f32[512,256]{1,0:T(8,128)S(1)}, f32[512,256]{1,0:T(8,128)}, u32[]{:S(2)}, u32[]{:S(2)}) %collective-permute-start.44) | collective-permute-done | bytes 524320 | tf_op jit(solution)/shard_map/ppermute | solution.py:446
  84.1 3.2 collective-permute-start.48
  90.2 24.2 %panel_b.1 = (bf16[1024,1024]{1,0:T(8,128)(2,1)}, bf16[1024,1024]{1,0:T(8,128)(2,1)}, bf16[128,256]{1,0:T(8,128)(2,1)}) custom-call(f32[512,256]{1,0:T(8,128)} %copy-done.10, f32[512,256]{1,0:T(8,128)} %collective-permute-done.43.refs_1_, f32[512,256]{1,0:T(8,128)} %collective-permute-done.44.refs_2_, f32[512,256]{1,0:T(8,128)} %collective-permute-done.45.refs_3_, ...), custom_call_target="tpu_custom_call" | custom-call | flops 32000000000 | bytes 8000000 | tf_op jit(solution)/shard_map/panel_b/pallas_call | solution.py:449
  115.7 3.3 collective-permute-start.50
  120.5 2.6 collective-permute-done.49.refs_3_
  123.1 2.6 fusion
  125.8 2.7 collective-permute-start.52
  132.0 24.5 %panel_c.1 = (bf16[512,1024]{1,0:T(8,128)(2,1)}, f32[512,512]{1,0:T(8,128)}, bf16[128,256]{1,0:T(8,128)(2,1)}) custom-call(f32[512,384]{1,0:T(8,128)} %slice.70.refs_0_, f32[512,384]{1,0:T(8,128)} %copy-done.26, f32[512,384]{1,0:T(8,128)} %copy-done.27, f32[512,384]{1,0:T(8,128)} %copy-done.28, bf16[1024,1024]{1,0:T(8,128)(2,1)} %get-tuple-element.154.refs_4_, ...), custom_call_target="tpu_custom_call" | custom-call | flops 35000000512 | bytes 8000000 | tf_op jit(solution)/shard_map/panel_c/pallas_call | solution.py:449
  157.6 5.0 %first_rows.1.refs_8_ = bf16[2,96,1024]{2,1,0:T(8,128)(2,1)} custom-call(f32[192,512]{1,0:T(8,128)} %bitcast.36, f32[192,512]{1,0:T(8,128)} %copy-done.2, f32[192,512]{1,0:T(8,128)} %copy-done.3, f32[192,512]{1,0:T(8,128)} %copy-done.4, bf16[1024,1024]{1,0:T(8,128)(2,1)} %get-tuple-element.154.refs_4_, bf16[1024,1024]{1,0:T(8,128)(2,1)} %get-tuple-element.155.refs_5_), custom_call_target="tpu_custom_call" | custom-call | flops 1200000000 | bytes 8000000 | tf_op jit(solution)/shard_map/first_rows/pallas_call | solution.py:449
  162.6 30.8 %panel_d.1 = (bf16[512,1024]{1,0:T(8,128)(2,1)}, bf16[1024,1024]{1,0:T(8,128)(2,1)}, bf16[1024,1024]{1,0:T(8,128)(2,1)}, bf16[128,256]{1,0:T(8,128)(2,1)}) custom-call(f32[4,128,512]{2,1,0:T(8,128)} %bitcast.47, f32[4,128,512]{2,1,0:T(8,128)} %collective-permute-done.46.refs_1_, f32[4,128,512]{2,1,0:T(8,128)} %collective-permute-done.54.refs_2_, ...), custom_call_target="tpu_custom_call" | custom-call | flops 38000001024 | bytes 8000000 | tf_op jit(solution)/shard_map/panel_d/pallas_call | solution.py:449
  193.4 6.8 %second_rows.1 = bf16[2,96,1024]{2,1,0:T(8,128)(2,1)} custom-call(f32[192,512]{1,0:T(8,128)} %bitcast.37, f32[192,512]{1,0:T(8,128)} %copy-done.2, f32[192,512]{1,0:T(8,128)} %copy-done.3, f32[192,512]{1,0:T(8,128)} %copy-done.4, bf16[1024,1024]{1,0:T(8,128)(2,1)} %get-tuple-element.175.refs_4_.whi, bf16[1024,1024]{1,0:T(8,128)(2,1)} %get-tuple-element.176.refs_5_.wlo, ...), custom_call_target="tpu_custom_call" | custom-call | flops 1700000000 | bytes 8000000 | tf_op jit(solution)/shard_map/second_rows/pallas_call | solution.py:449
  201.8 11.9 %columns_first.1 = (bf16[1024,768]{1,0:T(8,128)(2,1)}, bf16[1024,768]{1,0:T(8,128)(2,1)}, bf16[1024,768]{1,0:T(8,128)(2,1)}) custom-call(f32[2,256,768]{2,1,0:T(8,128)} %copy-done.6, f32[2,256,768]{2,1,0:T(8,128)} %collective-permute-done.50.refs_1_, f32[2,256,768]{2,1,0:T(8,128)} %bitcast.44, f32[2,256,768]{2,1,0:T(8,128)} %copy-done.25, ...), custom_call_target="tpu_custom_call" | custom-call | flops 8999999488 | bytes 8000000 | tf_op jit(solution)/shard_map/columns_first/pallas_call | solution.py:449
  213.9 2.6 collective-permute-start.59
  218.6 7.5 %columns_second.1.refs_5_ = bf16[1024,768]{1,0:T(8,128)(2,1)} custom-call(bf16[1024,768]{1,0:T(8,128)(2,1)} %get-tuple-element.185.nhi, bf16[1024,768]{1,0:T(8,128)(2,1)} %get-tuple-element.186.nlo, bf16[1024,1024]{1,0:T(8,128)(2,1)} %get-tuple-element.175.refs_4_.whi, bf16[1024,1024]{1,0:T(8,128)(2,1)} %get-tuple-element.176.refs_5_.wlo), custom_call_target="tpu_custom_call" | custom-call | flops 8999999488 | bytes 8000000 | tf_op jit(solution)/shard_map/columns_second/pallas_call | solution.py:449
  226.2 6.9 %collective-permute-done.59.refs_2_ = bf16[2,96,1024]{2,1,0:T(8,128)(2,1)S(1)} collective-permute-done((bf16[2,96,1024]{2,1,0:T(8,128)(2,1)S(1)}, bf16[2,96,1024]{2,1,0:T(8,128)(2,1)S(1)}, u32[]{:S(2)}, u32[]{:S(2)}) %collective-permute-start.59) | collective-permute-done | bytes 393248 | tf_op jit(solution)/shard_map/ppermute | solution.py:446
  236.4 6.8 %update.2 = (bf16[768,768]{1,0:T(8,128)(2,1)S(1)}, bf16[768,256]{1,0:T(8,128)(2,1)}) custom-call(bf16[8,2,96,1024]{3,2,1,0:T(8,128)(2,1)} %bitcast.31, bf16[2,96,1024]{2,1,0:T(8,128)(2,1)} %copy-done.1, bf16[2,96,1024]{2,1,0:T(8,128)(2,1)} %copy-done.13, bf16[2,96,1024]{2,1,0:T(8,128)(2,1)} %copy-done.14, bf16[2,96,1024]{2,1,0:T(8,128)(2,1)} %copy-done.15, ...), custom_call_target="tpu_custom_call" | custom-call | flops 2500000000 | bytes 9000000 | tf_op jit(solution)/shard_map/update/pallas_call | solution.py:597
  243.3 2.6 collective-permute-start.62
  249.4 32.1 %conditional.2 = (bf16[768,768]{1,0:T(8,128)(2,1)}) conditional(s32[]{:T(128)} %clamp.4, () %tuple.122, bf16[768,768]{1,0:T(8,128)(2,1)S(1)} %get-tuple-element.189.refs_0_, bf16[768,768]{1,0:T(8,128)(2,1)S(1)} %get-tuple-element.189.refs_0_, bf16[768,768]{1,0:T(8,128)(2,1)S(1)} %get-tuple-element.189.refs_0_, ...), branch_computations={%region_1.2_spmd, %region_2.3_spmd, %region_3.4_spmd, %region_4.5_... | conditional | bytes 4718640 | solution.py:468
  249.4 5.5 %collective-permute-start.12 = (bf16[768,768]{1,0:T(8,128)(2,1)S(1)}, bf16[768,768]{1,0:T(8,128)(2,1)}, u32[]{:S(2)}, u32[]{:S(2)}) collective-permute-start(bf16[768,768]{1,0:T(8,128)(2,1)S(1)} %param.13), channel_id=1, source_target_pairs={{0,64},{64,0},{96,32},{1,65},{65,1},{97,33},{2,66},{66,2},{98,34},... | collective-permute-start | bytes 3538952 | tf_op jit(solution)/shard_map/cond/branch_13_fun/ppermute | solution.py:466
  254.9 26.4 %collective-permute-done.12 = bf16[768,768]{1,0:T(8,128)(2,1)} collective-permute-done((bf16[768,768]{1,0:T(8,128)(2,1)S(1)}, bf16[768,768]{1,0:T(8,128)(2,1)}, u32[]{:S(2)}, u32[]{:S(2)}) %collective-permute-start.12) | collective-permute-done | bytes 1179680 | tf_op jit(solution)/shard_map/cond/branch_13_fun/ppermute | solution.py:466
  282.3 7.0 %update.3 = (bf16[768,768]{1,0:T(8,128)(2,1)}, bf16[768,256]{1,0:T(8,128)(2,1)}) custom-call(bf16[8,2,96,1024]{3,2,1,0:T(8,128)(2,1)} %bitcast.32, bf16[2,96,1024]{2,1,0:T(8,128)(2,1)} %copy-done, bf16[2,96,1024]{2,1,0:T(8,128)(2,1)} %copy-done.11, bf16[2,96,1024]{2,1,0:T(8,128)(2,1)} %copy-done.12, bf16[2,96,1024]{2,1,0:T(8,128)(2,1)} %collective-permute-done.63.refs_3_, ...), custom_call_target="tpu_custom_call" | custom-call | flops 2500000000 | bytes 9000000 | tf_op jit(solution)/shard_map/update/pallas_call | solution.py:597
  289.5 32.1 %conditional.3 = (bf16[768,768]{1,0:T(8,128)(2,1)}) conditional(s32[]{:T(128)} %clamp.4, () %tuple.125, bf16[768,768]{1,0:T(8,128)(2,1)} %get-tuple-element.196.refs_1_, bf16[768,768]{1,0:T(8,128)(2,1)} %get-tuple-element.196.refs_1_, bf16[768,768]{1,0:T(8,128)(2,1)} %get-tuple-element.196.refs_1_, ...), branch_computations={%region_17.18_spmd, %region_18.19_spmd, %region_19.20_spmd, %regio... | conditional | bytes 4718640 | solution.py:468
  291.6 30.0 %collective-permute-done.27 = bf16[768,768]{1,0:T(8,128)(2,1)} collective-permute-done((bf16[768,768]{1,0:T(8,128)(2,1)}, bf16[768,768]{1,0:T(8,128)(2,1)}, u32[]{:S(2)}, u32[]{:S(2)}) %collective-permute-start.27) | collective-permute-done | bytes 1179680 | tf_op jit(solution)/shard_map/cond/branch_13_fun/ppermute | solution.py:466
  327.4 8.9 %merge.1 = f32[2048,1024]{1,0:T(8,128)} custom-call(s32[4]{0:T(128)} %owner.1, s32[4,48]{1,0:T(4,128)} %block_map.1, bf16[2048,1024]{1,0:T(8,128)(2,1)} %bitcast.35, bf16[768,768]{1,0:T(8,128)(2,1)S(1)} %get-tuple-element.189.refs_0_, bf16[768,768]{1,0:T(8,128)(2,1)} %get-tuple-element.196.refs_1_, bf16[768,768]{1,0:T(8,128)(2,1)} %copy-done.7, ...), custom_call_target="tpu_custom_call" | custom-call | flops 10000000 | bytes 22000000 | tf_op jit(solution)/shard_map/merge/pallas_call | solution.py:638
  (162 shorter events, 59.1 us)
Async XLA Ops:
  7.2 76.8 %all-gather.7.cloned.1.call-start = ((), (), s32[]{:S(2)}) async-start(), calls=%async_computation | async-start | bytes 1310720 | tf_op jit(solution)/shard_map/all_gather | solution.py:493
  33.3 20.9 %collective-permute-start.38 = (f32[128,640]{1,0:T(8,128)S(1)}, f32[128,640]{1,0:T(8,128)S(1)}, u32[]{:S(2)}, u32[]{:S(2)}) collective-permute-start(f32[128,640]{1,0:T(8,128)S(1)} %get-tuple-element.214), channel_id=1, source_target_pairs={{0,8},{1,9},{2,10},{3,11},{4,12},{5,13},{6,14},{7,15},{8,0},{9,1},... | collective-permute-start | bytes 983048 | tf_op jit(solution)/shard_map/ppermute | solution.py:446
  35.1 19.1 %collective-permute-start.39 = (f32[128,640]{1,0:T(8,128)S(1)}, f32[128,640]{1,0:T(8,128)S(1)}, u32[]{:S(2)}, u32[]{:S(2)}) collective-permute-start(f32[128,640]{1,0:T(8,128)S(1)} %get-tuple-element.214), channel_id=1, source_target_pairs={{0,16},{1,17},{2,18},{3,19},{4,20},{5,21},{6,22},{7,23},{8,24},{9,... | collective-permute-start | bytes 983048 | tf_op jit(solution)/shard_map/ppermute | solution.py:446
  36.0 120.6 %all-gather.9.cloned.1.call-start = ((), (), s32[]{:S(2)}) async-start(), calls=%async_computation.1 | async-start | bytes 2359296 | tf_op jit(solution)/shard_map/all_gather | solution.py:512
  37.0 18.0 %collective-permute-start.40 = (f32[128,640]{1,0:T(8,128)S(1)}, f32[128,640]{1,0:T(8,128)S(1)}, u32[]{:S(2)}, u32[]{:S(2)}) collective-permute-start(f32[128,640]{1,0:T(8,128)S(1)} %get-tuple-element.214), channel_id=1, source_target_pairs={{0,24},{1,25},{2,26},{3,27},{4,28},{5,29},{6,30},{7,31},{8,16},{9,... | collective-permute-start | bytes 983048 | tf_op jit(solution)/shard_map/ppermute | solution.py:446
  56.1 17.8 %collective-permute-start.43 = (f32[512,256]{1,0:T(8,128)S(1)}, f32[512,256]{1,0:T(8,128)}, u32[]{:S(2)}, u32[]{:S(2)}) collective-permute-start(f32[512,256]{1,0:T(8,128)S(1)} %slice.75.refs_0_), channel_id=1, source_target_pairs={{0,1},{1,0},{2,3},{3,2},{4,5},{5,4},{6,7},{7,6},{8,9},{9,8},{10,11... | collective-permute-start | bytes 1572872 | tf_op jit(solution)/shard_map/ppermute | solution.py:446
  56.2 27.1 %collective-permute-start.44 = (f32[512,256]{1,0:T(8,128)S(1)}, f32[512,256]{1,0:T(8,128)}, u32[]{:S(2)}, u32[]{:S(2)}) collective-permute-start(f32[512,256]{1,0:T(8,128)S(1)} %slice.75.refs_0_), channel_id=1, source_target_pairs={{0,2},{1,3},{2,0},{3,1},{4,6},{5,7},{6,4},{7,5},{8,10},{9,11},{10,... | collective-permute-start | bytes 1572872 | tf_op jit(solution)/shard_map/ppermute | solution.py:446
  58.1 25.8 %collective-permute-start.45 = (f32[512,256]{1,0:T(8,128)S(1)}, f32[512,256]{1,0:T(8,128)}, u32[]{:S(2)}, u32[]{:S(2)}) collective-permute-start(f32[512,256]{1,0:T(8,128)S(1)} %slice.75.refs_0_), channel_id=1, source_target_pairs={{0,3},{1,2},{2,1},{3,0},{4,7},{5,6},{6,5},{7,4},{8,11},{9,10},{10,... | collective-permute-start | bytes 1572872 | tf_op jit(solution)/shard_map/ppermute | solution.py:446
  60.8 23.1 %collective-permute-start.41 = (f32[2,384,256]{2,1,0:T(8,128)}, f32[2,384,256]{2,1,0:T(8,128)}, u32[]{:S(2)}, u32[]{:S(2)}) collective-permute-start(f32[2,384,256]{2,1,0:T(8,128)} %get-tuple-element.138), channel_id=1, source_target_pairs={{0,4},{1,5},{2,6},{3,7},{4,0},{5,1},{6,2},{7,3},{8,12},{9,13},{10,... | collective-permute-start | bytes 2359304 | tf_op jit(solution)/shard_map/ppermute | solution.py:446
  61.1 22.8 %collective-permute-start.42 = (f32[256,768]{1,0:T(8,128)S(1)}, f32[256,768]{1,0:T(8,128)}, u32[]{:S(2)}, u32[]{:S(2)}) collective-permute-start(f32[256,768]{1,0:T(8,128)S(1)} %get-tuple-element.139), channel_id=1, source_target_pairs={{0,16},{1,17},{2,18},{3,19},{4,20},{5,21},{6,22},{7,23},{8,24},{9,... | collective-permute-start | bytes 2359304 | tf_op jit(solution)/shard_map/ppermute | solution.py:446
  61.7 174.0 %all-gather.11.cloned.1.call-start = ((), (), s32[]{:S(2)}) async-start(), calls=%async_computation.2 | async-start | bytes 3538944 | tf_op jit(solution)/shard_map/all_gather | solution.py:556
  83.9 31.7 %collective-permute-start.47 = (f32[512,384]{1,0:T(8,128)}, f32[512,384]{1,0:T(8,128)S(1)}, u32[]{:S(2)}, u32[]{:S(2)}) collective-permute-start(f32[512,384]{1,0:T(8,128)} %slice.70.refs_0_), channel_id=1, source_target_pairs={{0,1},{1,0},{2,3},{3,2},{4,5},{5,4},{6,7},{7,6},{8,9},{9,8},{10,11... | collective-permute-start | bytes 2359304 | tf_op jit(solution)/shard_map/ppermute | solution.py:446
  84.1 36.5 %collective-permute-start.48 = (f32[512,384]{1,0:T(8,128)}, f32[512,384]{1,0:T(8,128)S(1)}, u32[]{:S(2)}, u32[]{:S(2)}) collective-permute-start(f32[512,384]{1,0:T(8,128)} %slice.70.refs_0_), channel_id=1, source_target_pairs={{0,2},{1,3},{2,0},{3,1},{4,6},{5,7},{6,4},{7,5},{8,10},{9,11},{10,... | collective-permute-start | bytes 2359304 | tf_op jit(solution)/shard_map/ppermute | solution.py:446
  87.3 35.8 %collective-permute-start.49 = (f32[512,384]{1,0:T(8,128)}, f32[512,384]{1,0:T(8,128)S(1)}, u32[]{:S(2)}, u32[]{:S(2)}) collective-permute-start(f32[512,384]{1,0:T(8,128)} %slice.70.refs_0_), channel_id=1, source_target_pairs={{0,3},{1,2},{2,1},{3,0},{4,7},{5,6},{6,5},{7,4},{8,11},{9,10},{10,... | collective-permute-start | bytes 2359304 | tf_op jit(solution)/shard_map/ppermute | solution.py:446
  88.7 34.4 %collective-permute-start.46 = (f32[4,128,512]{2,1,0:T(8,128)}, f32[4,128,512]{2,1,0:T(8,128)}, u32[]{:S(2)}, u32[]{:S(2)}) collective-permute-start(f32[4,128,512]{2,1,0:T(8,128)} %bitcast.45), channel_id=1, source_target_pairs={{0,8},{1,9},{2,10},{3,11},{4,12},{5,13},{6,14},{7,15},{8,0},{9,1},... | collective-permute-start | bytes 3145736 | tf_op jit(solution)/shard_map/ppermute | solution.py:446
  89.2 41.4 %collective-permute-start.54 = (f32[4,128,512]{2,1,0:T(8,128)}, f32[4,128,512]{2,1,0:T(8,128)}, u32[]{:S(2)}, u32[]{:S(2)}) collective-permute-start(f32[4,128,512]{2,1,0:T(8,128)} %bitcast.46), channel_id=1, source_target_pairs={{0,16},{1,17},{2,18},{3,19},{4,20},{5,21},{6,22},{7,23},{8,24},{9,... | collective-permute-start | bytes 3145736 | tf_op jit(solution)/shard_map/ppermute | solution.py:446
  115.7 40.9 %collective-permute-start.50 = (f32[2,256,768]{2,1,0:T(8,128)S(1)}, f32[2,256,768]{2,1,0:T(8,128)}, u32[]{:S(2)}, u32[]{:S(2)}) collective-permute-start(f32[2,256,768]{2,1,0:T(8,128)S(1)} %pad_maximum_fusion.refs_0_), channel_id=1, source_target_pairs={{0,8},{1,9},{2,10},{3,11},{4,12},{5,13},{6,14},{7,15},{8,0},{9,1},... | collective-permute-start | bytes 4718600 | tf_op jit(solution)/shard_map/ppermute | solution.py:446
  125.8 30.8 %collective-permute-start.51 = (f32[192,512]{1,0:T(8,128)}, f32[192,512]{1,0:T(8,128)S(1)}, u32[]{:S(2)}, u32[]{:S(2)}) collective-permute-start(f32[192,512]{1,0:T(8,128)} %bitcast.10), channel_id=1, source_target_pairs={{0,1},{1,0},{2,3},{3,2},{4,5},{5,4},{6,7},{7,6},{8,9},{9,8},{10,11... | collective-permute-start | bytes 1179656 | tf_op jit(solution)/shard_map/ppermute | solution.py:446
  125.8 30.7 %collective-permute-start.52 = (f32[192,512]{1,0:T(8,128)S(1)}, f32[192,512]{1,0:T(8,128)S(1)}, u32[]{:S(2)}, u32[]{:S(2)}) collective-permute-start(f32[192,512]{1,0:T(8,128)S(1)} %bitcast.41), channel_id=1, source_target_pairs={{0,2},{1,3},{2,0},{3,1},{4,6},{5,7},{6,4},{7,5},{8,10},{9,11},{10,... | collective-permute-start | bytes 1179656 | tf_op jit(solution)/shard_map/ppermute | solution.py:446
  128.6 28.0 %collective-permute-start.53 = (f32[192,512]{1,0:T(8,128)S(1)}, f32[192,512]{1,0:T(8,128)S(1)}, u32[]{:S(2)}, u32[]{:S(2)}) collective-permute-start(f32[192,512]{1,0:T(8,128)S(1)} %bitcast.40), channel_id=1, source_target_pairs={{0,3},{1,2},{2,1},{3,0},{4,7},{5,6},{6,5},{7,4},{8,11},{9,10},{10,... | collective-permute-start | bytes 1179656 | tf_op jit(solution)/shard_map/ppermute | solution.py:446
  130.5 26.1 %collective-permute-start.55 = (f32[4,128,512]{2,1,0:T(8,128)}, f32[4,128,512]{2,1,0:T(8,128)}, u32[]{:S(2)}, u32[]{:S(2)}) collective-permute-start(f32[4,128,512]{2,1,0:T(8,128)} %collective-permute-done.46.refs_1_), channel_id=1, source_target_pairs={{0,16},{1,17},{2,18},{3,19},{4,20},{5,21},{6,22},{7,23},{8,24},{9,... | collective-permute-start | bytes 3145736 | tf_op jit(solution)/shard_map/ppermute | solution.py:446
  156.6 36.8 %collective-permute-start.56 = (f32[2,256,768]{2,1,0:T(8,128)}, f32[2,256,768]{2,1,0:T(8,128)S(1)}, u32[]{:S(2)}, u32[]{:S(2)}) collective-permute-start(f32[2,256,768]{2,1,0:T(8,128)} %bitcast.43), channel_id=1, source_target_pairs={{0,16},{1,17},{2,18},{3,19},{4,20},{5,21},{6,22},{7,23},{8,24},{9,... | collective-permute-start | bytes 4718600 | tf_op jit(solution)/shard_map/ppermute | solution.py:446
  200.2 13.5 %collective-permute-start.57 = (bf16[2,96,1024]{2,1,0:T(8,128)(2,1)}, bf16[2,96,1024]{2,1,0:T(8,128)(2,1)S(1)}, u32[]{:S(2)}, u32[]{:S(2)}) collective-permute-start(bf16[2,96,1024]{2,1,0:T(8,128)(2,1)} %second_rows.1), channel_id=1, source_target_pairs={{0,4},{1,5},{2,6},{3,7},{4,0},{5,1},{6,2},{7,3},{8,12},{9,13},{10,... | collective-permute-start | bytes 1179656 | tf_op jit(solution)/shard_map/ppermute | solution.py:446
  213.9 19.2 %collective-permute-start.59 = (bf16[2,96,1024]{2,1,0:T(8,128)(2,1)S(1)}, bf16[2,96,1024]{2,1,0:T(8,128)(2,1)S(1)}, u32[]{:S(2)}, u32[]{:S(2)}) collective-permute-start(bf16[2,96,1024]{2,1,0:T(8,128)(2,1)S(1)} %pad_maximum_fusion.2.refs_0_), channel_id=1, source_target_pairs={{0,2},{1,3},{2,0},{3,1},{4,6},{5,7},{6,4},{7,5},{8,10},{9,11},{10,... | collective-permute-start | bytes 1179656 | tf_op jit(solution)/shard_map/ppermute | solution.py:446
  216.5 19.2 %collective-permute-start.60 = (bf16[2,96,1024]{2,1,0:T(8,128)(2,1)S(1)}, bf16[2,96,1024]{2,1,0:T(8,128)(2,1)S(1)}, u32[]{:S(2)}, u32[]{:S(2)}) collective-permute-start(bf16[2,96,1024]{2,1,0:T(8,128)(2,1)S(1)} %pad_maximum_fusion.2.refs_0_), channel_id=1, source_target_pairs={{0,3},{1,2},{2,1},{3,0},{4,7},{5,6},{6,5},{7,4},{8,11},{9,10},{10,... | collective-permute-start | bytes 1179656 | tf_op jit(solution)/shard_map/ppermute | solution.py:446
  243.3 38.2 %collective-permute-start.61 = (bf16[2,96,1024]{2,1,0:T(8,128)(2,1)S(1)}, bf16[2,96,1024]{2,1,0:T(8,128)(2,1)S(1)}, u32[]{:S(2)}, u32[]{:S(2)}) collective-permute-start(bf16[2,96,1024]{2,1,0:T(8,128)(2,1)S(1)} %pad_maximum_fusion.3.refs_0_), channel_id=1, source_target_pairs={{0,1},{1,0},{2,3},{3,2},{4,5},{5,4},{6,7},{7,6},{8,9},{9,8},{10,11... | collective-permute-start | bytes 1179656 | tf_op jit(solution)/shard_map/ppermute | solution.py:446
  243.3 38.2 %collective-permute-start.62 = (bf16[2,96,1024]{2,1,0:T(8,128)(2,1)S(1)}, bf16[2,96,1024]{2,1,0:T(8,128)(2,1)S(1)}, u32[]{:S(2)}, u32[]{:S(2)}) collective-permute-start(bf16[2,96,1024]{2,1,0:T(8,128)(2,1)S(1)} %pad_maximum_fusion.3.refs_0_), channel_id=1, source_target_pairs={{0,2},{1,3},{2,0},{3,1},{4,6},{5,7},{6,4},{7,5},{8,10},{9,11},{10,... | collective-permute-start | bytes 1179656 | tf_op jit(solution)/shard_map/ppermute | solution.py:446
  245.9 35.6 %collective-permute-start.63 = (bf16[2,96,1024]{2,1,0:T(8,128)(2,1)S(1)}, bf16[2,96,1024]{2,1,0:T(8,128)(2,1)}, u32[]{:S(2)}, u32[]{:S(2)}) collective-permute-start(bf16[2,96,1024]{2,1,0:T(8,128)(2,1)S(1)} %pad_maximum_fusion.3.refs_0_), channel_id=1, source_target_pairs={{0,3},{1,2},{2,1},{3,0},{4,7},{5,6},{6,5},{7,4},{8,11},{9,10},{10,... | collective-permute-start | bytes 1179656 | tf_op jit(solution)/shard_map/ppermute | solution.py:446
  249.3 73.0 %collective-permute-start.64 = (bf16[768,768]{1,0:T(8,128)(2,1)S(1)}, bf16[768,768]{1,0:T(8,128)(2,1)S(1)}, u32[]{:S(2)}, u32[]{:S(2)}) collective-permute-start(bf16[768,768]{1,0:T(8,128)(2,1)S(1)} %get-tuple-element.189.refs_0_), channel_id=1, source_target_pairs={{0,32},{32,0},{64,96},{96,64},{1,33},{33,1},{65,97},{97,65},{2,34}... | collective-permute-start | bytes 3538952 | tf_op jit(solution)/shard_map/ppermute | solution.py:461
  249.4 31.8 %collective-permute-start.12 = (bf16[768,768]{1,0:T(8,128)(2,1)S(1)}, bf16[768,768]{1,0:T(8,128)(2,1)}, u32[]{:S(2)}, u32[]{:S(2)}) collective-permute-start(bf16[768,768]{1,0:T(8,128)(2,1)S(1)} %param.13), channel_id=1, source_target_pairs={{0,64},{64,0},{96,32},{1,65},{65,1},{97,33},{2,66},{66,2},{98,34},... | collective-permute-start | bytes 3538952 | tf_op jit(solution)/shard_map/cond/branch_13_fun/ppermute | solution.py:466
  289.4 35.2 %collective-permute-start.65 = (bf16[768,768]{1,0:T(8,128)(2,1)}, bf16[768,768]{1,0:T(8,128)(2,1)}, u32[]{:S(2)}, u32[]{:S(2)}) collective-permute-start(bf16[768,768]{1,0:T(8,128)(2,1)} %get-tuple-element.196.refs_1_), channel_id=1, source_target_pairs={{0,32},{32,0},{64,96},{96,64},{1,33},{33,1},{65,97},{97,65},{2,34}... | collective-permute-start | bytes 3538952 | tf_op jit(solution)/shard_map/ppermute | solution.py:461
  289.6 32.0 %collective-permute-start.27 = (bf16[768,768]{1,0:T(8,128)(2,1)}, bf16[768,768]{1,0:T(8,128)(2,1)}, u32[]{:S(2)}, u32[]{:S(2)}) collective-permute-start(bf16[768,768]{1,0:T(8,128)(2,1)} %param.29), channel_id=1, source_target_pairs={{0,64},{64,0},{96,32},{1,65},{65,1},{97,33},{2,66},{66,2},{98,34},... | collective-permute-start | bytes 3538952 | tf_op jit(solution)/shard_map/cond/branch_13_fun/ppermute | solution.py:466
  (42 other events, 449.9 us)
Sparse Core Ops, SparseCore 0:
  36.1 27.8 all-gather.6
  65.6 36.1 all-gather.8
  162.7 43.5 all-gather.10
